TPU v7x, 512 devices: a whole 4x8x8 slice. The times are simulated.
512 devices in a mesh: grid: 32 (over z_hi, y), depth: 16 (over x, z_lo, core).
Axes of the slice: x: 4, y: 8, z: 8 (z_hi: 4, z_lo: 2; z = z_hi * 2 + z_lo), core: 2. Of those that a mesh axis runs over, the one named last changes fastest.
Arguments:
- amplitudes: bfloat16 [2, 32768, 1024], P(None, 'grid', 'depth'), may hold values from -6 to 6
- first_factor: bfloat16 [2, 1024, 512], P(None, 'depth'), may hold values from -0.1875 to 0.1875
- second_factor: bfloat16 [2, 1024, 512], replicated, may hold values from -0.125 to 0.125
Outputs:
- amplitude_block: bfloat16 [2, 1024, 16, 512], P(None, ('grid', 'depth'))
All inputs are finite; a program needn't handle non-finite values.
Results may differ from a plain program's by a relative error of at most 0.025.
Values may be sent and summed in bfloat16 or wider, within the bound.
A program may use at most 64 MiB of HBM per device.

v0:
```python
import jax
import jax.numpy as jnp
from jax import lax
from jax.sharding import PartitionSpec as P

JHI = 32
RLO = 32
JLO = 16


def complex_product(left, right):
    real_part = jnp.dot(left[0], right[0], preferred_element_type=jnp.float32) - jnp.dot(
        left[1], right[1], preferred_element_type=jnp.float32
    )
    imag_part = jnp.dot(left[0], right[1], preferred_element_type=jnp.float32) + jnp.dot(
        left[1], right[0], preferred_element_type=jnp.float32
    )
    return jnp.stack((real_part, imag_part), axis=0)


def on_device(amplitudes, first_factor, second_factor):
    devices = lax.axis_size("depth")
    row_count = amplitudes.shape[1]
    width_out = second_factor.shape[2]
    real_part = jnp.dot(
        amplitudes[0], first_factor[0], preferred_element_type=jnp.float32
    ) - jnp.dot(amplitudes[1], first_factor[1], preferred_element_type=jnp.float32)
    imag_part = jnp.dot(
        amplitudes[0], first_factor[1], preferred_element_type=jnp.float32
    ) + jnp.dot(amplitudes[1], first_factor[0], preferred_element_type=jnp.float32)
    terms = jnp.stack((real_part, imag_part), axis=1)
    summed = lax.psum_scatter(terms.astype(jnp.bfloat16), "depth", scatter_dimension=2, tiled=True)
    contracted = summed.reshape(row_count, 2, JHI // devices, JLO)
    moved = lax.all_to_all(contracted, "depth", split_axis=3, concat_axis=2, tiled=True)
    local_low = JLO // devices
    high_rows = row_count // RLO
    grouped = moved.reshape(high_rows, RLO, 2, JHI, local_low).transpose(2, 0, 4, 1, 3)
    grouped = grouped.reshape(2, high_rows * local_low, RLO * JHI)
    result = complex_product(grouped, second_factor)
    result = result.reshape(2, high_rows, local_low, width_out).astype(jnp.bfloat16)
    return lax.all_to_all(result, "depth", split_axis=1, concat_axis=2, tiled=True)


def solution(mesh):
    in_specs = (P(None, "grid", "depth"), P(None, "depth", None), P())
    out_specs = P(None, ("grid", "depth"), None, None)
    return jax.shard_map(
        on_device, mesh=mesh, in_specs=in_specs, out_specs=out_specs, check_vma=False
    )
```

profile of v0, /device:TPU:1, one launch (start us, length us, event | category | flops | bytes accessed | tf_op | source)
XLA Modules:
  0.0 186.3 jit_solution(16815809654339594279)
XLA Ops:
  6.5 1.4 fusion.20
  8.0 0.5 fusion.18
  8.4 0.5 fusion
  8.9 0.5 fusion.1
  9.4 0.2 pad_maximum_fusion
  9.6 4.0 %copy.26 = bf16[1024,2,512]{0,1,2:T(2,128)(2,1)} copy(bf16[1024,2,512]{2,0,1:T(8,128)(2,1)S(1)} %pad_maximum_fusion) | data formatting | bytes 4194304 | tf_op jit(solution)/shard_map/stack | solution.py:31
  13.6 1.4 dynamic-slice
  15.7 138.4 %all-reduce.3.cloned.1.call-done = bf16[1024,2,512]{0,1,2:T(2,128)(2,1)} async-done(((bf16[1024,2,512]{0,1,2:T(2,128)(2,1)}), bf16[1024,2,512]{0,1,2:T(2,128)(2,1)}) %all-reduce.3.cloned.1.call-update) | async-done | bytes 2097168
  154.1 1.0 constant_dynamic-slice_fusion
  155.1 0.1 copy.28
  155.2 11.8 %all_to_all.33 = bf16[1024,2,2,16]{0,2,1,3:T(2,128)(2,1)S(1)} all-to-all(bf16[1024,2,2,16]{0,2,1,3:T(2,128)(2,1)S(1)} %copy.28), channel_id=1, replica_groups=mesh['grid'=32,'depth'=16] {'depth'}, dimensions={3} | all-to-all | bytes 262144 | tf_op jit(solution)/shard_map/all_to_all | solution.py:34
  167.0 0.1 copy.29
  167.1 0.3 reshape.48
  167.4 0.3 copy.30
  167.8 0.3 squeeze.36
  168.1 0.3 fusion.10
  168.3 0.3 fusion.6
  168.6 0.4 copy.31
  169.0 0.3 squeeze.38
  169.2 0.3 fusion.5
  169.5 0.3 fusion.4
  169.8 0.1 copy.32
  169.9 8.9 %all_to_all.34 = bf16[2,32,1,512]{3,0,2,1:T(2,128)(2,1)S(1)} all-to-all(bf16[2,32,1,512]{3,0,2,1:T(2,128)(2,1)S(1)} %copy.32), channel_id=1, replica_groups=mesh['grid'=32,'depth'=16] {'depth'}, dimensions={1} | all-to-all | bytes 131072 | tf_op jit(solution)/shard_map/all_to_all | solution.py:41
  178.9 0.6 copy.33
  (10 shorter events, 0.1 us)
Async XLA Ops:
  6.5 1.4 copy-start.1
  6.5 1.4 copy-start.2
  6.5 147.5 %all-reduce.3.cloned.1.call-start = ((), (), s32[]{:S(2)}) async-start(), calls=%async_computation.2 | async-start | bytes 4194304
  13.6 154.4 %copy-start = (bf16[2,1024,512]{2,1,0:T(8,128)(2,1)S(1)}, bf16[2,1024,512]{2,1,0:T(8,128)(2,1)}, u32[]{:S(2)}) copy-start(bf16[2,1024,512]{2,1,0:T(8,128)(2,1)} %param.5) | copy-start | bytes 6291460
Sparse Core Ops, SparseCore 0:
  13.7 140.2 all-reduce.2
where the time goes:
time: 187 us; the launch traced here: 186 us
  waiting for transfers between devices  138 us (74%)
  blocking collectives  20.8 us (11%)
  between operations  14.1 us (8%)
  local copies, waits for them, and re-layouts  8.92 us (5%)
  matrix products  3.93 us (2%)
    unnamed x2, waiting for transfers between devices  138 us
    all_to_all x1, blocking collectives, on_device(): lax.all_to_all(contracted, 'depth', split_axis=3, concat_axis=2, tiled=True)  11.8 us
    all_to_all x1, blocking collectives, on_device(): lax.all_to_all(result, 'depth', split_axis=1, concat_axis=2, tiled=True)  8.94 us
    another operation x1, local copies, waits for them, and re-layouts, on_device(): terms = jnp.stack((real_part, imag_part), axis=1)  4.02 us
  transfers between devices with their start and end apart: 1, of which 1 were waited for; matrix products, arithmetic and copies ran while one was open for 1% of the time, Pallas kernels for 0%

commit v1 on v0

v1 whole, which is shorter than its diff:
```python
import jax
import jax.numpy as jnp
from jax import lax
from jax.experimental import pallas as pl
from jax.experimental.pallas import tpu as pltpu
from jax.sharding import PartitionSpec as P

MESH = pl.DeviceIdType.MESH
XS = 4
JHI = 32
RLO = 32
JLO = 16
J = JHI * JLO
G2 = RLO * JHI
M = 512
KH = 64
KB = 128
ROWS = 128
CHUNKS = 4
CJ = J // CHUNKS
HJ = J // 2
F32 = jnp.float32
BF16 = jnp.bfloat16


def kernel(at_ref, ff_ref, sf_ref, out_ref,
           s_vmem, abuf, bbuf, bt, wbuf, acc, half_send, half_recv, z_send, z_recv, lhs,
           local_sem, a_sems, x_sems, half_sems, z_sems):
    grid = lax.axis_index("grid")
    depth = lax.axis_index("depth")
    x = depth // 4
    zl = (depth // 2) % 2
    core = depth % 2

    def device(dx):
        return grid, (lax.rem(x + dx, XS) * 2 + zl) * 2 + core

    xp, xm, x2 = device(1), device(3), device(2)
    zp = (grid, (x * 2 + 1 - zl) * 2 + core)
    sibling = (grid, (x * 2 + zl) * 2 + 1 - core)
    partners = (xp, xm, x2, zp, sibling)

    barrier = pltpu.get_barrier_semaphore()
    for partner in partners:
        pl.semaphore_signal(barrier, inc=1, device_id=partner, device_id_type=MESH)

    def rows_of(dx, z):
        return pl.ds(pl.multiple_of((lax.rem(x + dx, XS) * 2 + z) * ROWS, ROWS), ROWS)

    z_of = (1 - zl, zl)
    load_b = pltpu.make_async_copy(ff_ref, bbuf.at[0], local_sem.at[0])
    load_a = [pltpu.make_async_copy(at_ref.at[:, :, rows_of(0, z_of[s])], abuf.at[s, 0], local_sem.at[1 + s])
              for s in range(2)]
    load_s = pltpu.make_async_copy(sf_ref, s_vmem, local_sem.at[3])

    def remote(src, dst, sems, i, to):
        return pltpu.make_async_remote_copy(
            src_ref=src, dst_ref=dst, send_sem=sems.at[0, i], recv_sem=sems.at[1, i],
            device_id=to, device_id_type=MESH)

    halves = [pl.ds(h * HJ, HJ) for h in range(2)]
    from_xm = [remote(ff_ref.at[:, :, halves[h]], bbuf.at[1, :, :, halves[h]], x_sems, h, xp) for h in range(2)]
    from_xp = [remote(ff_ref.at[:, :, halves[h]], bbuf.at[3, :, :, halves[h]], x_sems, 2 + h, xm) for h in range(2)]
    relay_p = [remote(bbuf.at[1, 0, :, halves[h]], bbuf.at[2, 0, :, halves[h]], x_sems, 4 + h, xp) for h in range(2)]
    relay_m = [remote(bbuf.at[3, 1, :, halves[h]], bbuf.at[2, 1, :, halves[h]], x_sems, 6 + h, xm) for h in range(2)]

    a_copies = [{dx: remote(at_ref.at[:, :, rows_of(dx, z_of[s])], abuf.at[s, dx], a_sems, s * 3 + dx - 1, device(dx))
                 for dx in (1, 3, 2)} for s in range(2)]

    pl.semaphore_wait(barrier, len(partners))
    from_xm[0].start()
    from_xp[0].start()
    for copy in a_copies[0].values():
        copy.start()
    load_b.start()
    load_a[0].start()
    from_xm[1].start()
    from_xp[1].start()
    load_a[1].start()
    load_s.start()

    def transpose(slot, h):
        bt[halves[h], pl.ds(slot * KB, KB)] = bbuf[slot, :, :, halves[h]].reshape(KB, HJ).T

    lo = lax.broadcasted_iota(jnp.int32, (KB, ROWS), 1) < 64

    def weights(s):
        load_a[s].wait()
        for copy in a_copies[s].values():
            copy.wait_recv()
        for slot in range(XS):
            real = abuf[s, slot, 0].astype(F32)
            imag = abuf[s, slot, 1].astype(F32)
            for_real = jnp.concatenate([real, -imag], axis=0)
            for_imag = jnp.concatenate([imag, real], axis=0)
            first = jnp.where(lo, for_real, pltpu.roll(for_imag, 64, 1))
            second = jnp.where(lo, pltpu.roll(for_real, 64, 1), for_imag)
            mine = jnp.where(core == 0, first, second)
            other = jnp.where(core == 0, second, first)
            wbuf[s, pl.ds(slot * KB, KB)] = jnp.concatenate([mine, other], axis=1).astype(BF16)

    half_copies = [[], []]
    z_copies = []

    def contract(s, h):
        for chunk in range(2 * h, 2 * h + 2):
            where = pl.ds(chunk * CJ, CJ)
            total = jnp.dot(bt[where], wbuf[s], preferred_element_type=F32)
            acc[s, where] = total[:, :128]
            half_send[s, where] = total[:, 128:].astype(BF16)
            copy = remote(half_send.at[s, where], half_recv.at[s, where], half_sems, s * CHUNKS + chunk, sibling)
            copy.start()
            half_copies[s].append(copy)

    def send_z(h):
        for chunk in range(2 * h, 2 * h + 2):
            where = pl.ds(chunk * CJ, CJ)
            half_copies[0][chunk].wait_recv()
            z_send[where] = (acc[0, where] + half_recv[0, where].astype(F32)).astype(BF16)
            copy = remote(z_send.at[where], z_recv.at[where], z_sems, chunk, zp)
            copy.start()
            z_copies.append(copy)

    load_b.wait()
    transpose(0, 0)
    transpose(0, 1)
    from_xm[0].wait_recv()
    relay_p[0].start()
    from_xp[0].wait_recv()
    relay_m[0].start()
    for copy in a_copies[1].values():
        copy.start()
    transpose(1, 0)
    transpose(3, 0)
    weights(0)
    from_xm[1].wait_recv()
    relay_p[1].start()
    from_xp[1].wait_recv()
    relay_m[1].start()
    relay_p[0].wait_recv()
    relay_m[0].wait_recv()
    transpose(2, 0)
    contract(0, 0)
    transpose(1, 1)
    transpose(3, 1)
    send_z(0)
    relay_p[1].wait_recv()
    relay_m[1].wait_recv()
    transpose(2, 1)
    contract(0, 1)
    weights(1)
    send_z(1)
    contract(1, 0)
    contract(1, 1)

    sent = from_xm + from_xp + relay_p + relay_m + half_copies[0] + half_copies[1]
    for copies in a_copies:
        sent += list(copies.values())
    for copy in sent:
        copy.wait_send()

    def swap(v, tile_bit, lane_bit):
        step, width = 1 << tile_bit, 1 << lane_bit
        v = v.reshape(16 // (2 * step), 2, step, JLO, 128)
        a = v[:, 0].reshape(8, JLO, 128)
        b = v[:, 1].reshape(8, JLO, 128)
        low = (lax.broadcasted_iota(jnp.int32, a.shape, 2) // width) % 2 == 0
        a, b = (jnp.where(low, a, pltpu.roll(b, width, 2)), jnp.where(low, pltpu.roll(a, 128 - width, 2), b))
        shape = (16 // (2 * step), 1, step, JLO, 128)
        return jnp.concatenate([a.reshape(shape), b.reshape(shape)], axis=1).reshape(16, JLO, 128)

    load_s.wait()
    result = jnp.zeros((64, M), F32)
    for top in range(2):
        where = pl.ds(top * 256, 256)
        for chunk in range(2 * top, 2 * top + 2):
            half_copies[1][chunk].wait_recv()
            z_copies[chunk].wait_recv()
        value = acc[1, where] + half_recv[1, where].astype(F32) + z_recv[where].astype(F32)
        value = value.astype(BF16).reshape(16, JLO, 128)
        for tile_bit, lane_bit in ((0, 0), (1, 1), (2, 2), (3, 3), (3, 6), (2, 5)):
            value = swap(value, tile_bit, lane_bit)

        right = []
        for u in range(4):
            for p in range(2):
                at = pl.ds((u * 2 + p) * 128, 128)
                turned = pl.ds((u * 2 + 1 - p) * 128, 128)
                for rh in range(2):
                    block = value[p * 8 + rh * 4 + u]
                    lhs[top, pl.ds(rh * 16, 16), at] = block if p == 0 else -block
                    lhs[top, pl.ds(32 + rh * 16, 16), turned] = block
                for t in range(8):
                    rl = (t % 2) * 16 + (t // 4) * 8 + (t // 2 % 2) * 4 + u
                    right.append(s_vmem[p, pl.ds(rl * JHI + top * 16, 16)])
        result += jnp.dot(lhs[top], jnp.concatenate(right, axis=0), preferred_element_type=F32)
    out_ref[...] = result.astype(BF16).reshape(2, 2, JLO, M)

    for copy in z_copies:
        copy.wait_send()


def on_device(amplitudes, first_factor, second_factor):
    arguments = [pltpu.with_memory_space_constraint(a, pltpu.HBM)
                 for a in (jnp.swapaxes(amplitudes, 1, 2), first_factor, second_factor)]
    return pl.pallas_call(
        kernel,
        out_shape=pltpu.VMEM((2, 2, JLO, M), BF16),
        in_specs=[pl.BlockSpec(memory_space=pltpu.HBM)] * 3,
        out_specs=pl.BlockSpec(memory_space=pltpu.VMEM),
        scratch_shapes=[
            pltpu.VMEM((2, G2, M), BF16),
            pltpu.VMEM((2, XS, 2, KH, ROWS), BF16),
            pltpu.VMEM((XS, 2, KH, J), BF16),
            pltpu.VMEM((J, XS * KB), BF16),
            pltpu.VMEM((2, XS * KB, 256), BF16),
            pltpu.VMEM((2, J, 128), F32),
            pltpu.VMEM((2, J, 128), BF16),
            pltpu.VMEM((2, J, 128), BF16),
            pltpu.VMEM((J, 128), BF16),
            pltpu.VMEM((J, 128), BF16),
            pltpu.VMEM((2, 64, G2), BF16),
            pltpu.SemaphoreType.DMA((4,)),
            pltpu.SemaphoreType.DMA((2, 6)),
            pltpu.SemaphoreType.DMA((2, 8)),
            pltpu.SemaphoreType.DMA((2, 2 * CHUNKS)),
            pltpu.SemaphoreType.DMA((2, CHUNKS)),
        ],
        compiler_params=pltpu.CompilerParams(
            collective_id=0, has_side_effects=True, vmem_limit_bytes=32 * 1024 * 1024),
        cost_estimate=pl.CostEstimate(flops=800_000_000, bytes_accessed=2_600_000, transcendentals=0),
    )(*arguments)


def solution(mesh):
    return jax.shard_map(
        on_device, mesh=mesh,
        in_specs=(P(None, "grid", "depth"), P(None, "depth", None), P()),
        out_specs=P(None, ("grid", "depth"), None, None), check_vma=False)
```

time: 187 us -> 23.7 us (0.13)
  waiting for transfers between devices: 138 us -> 0 us
  Pallas kernels: 0 us -> 22.9 us
  blocking collectives: 20.8 us -> 0 us
  between operations: 14.1 us -> 0.01 us
  local copies, waits for them, and re-layouts: 8.92 us -> 0.63 us
  matrix products: 3.93 us -> 0 us
    unnamed x2 -> x0, waiting for transfers between devices: 138 us -> none
    pallas_call x0 -> x1, Pallas kernels: none -> 22.9 us  [on_device(): pl.pallas_call(kernel, out_shape=pltpu.VMEM((2, 2, JLO, M), BF16), in_spe...]
    all_to_all x2 -> x0, blocking collectives: 20.8 us -> none  [the longest x1 11.8 us: on_device(): lax.all_to_all(contracted, 'depth', split_axis=3, concat_axis=2, tiled=True)]
    another operation x2 -> x0, local copies, waits for them, and re-layouts: 4.09 us -> none  [the longest x1 4.02 us: on_device(): terms = jnp.stack((real_part, imag_part), axis=1)]
    dot_general x8 -> x0, matrix products: 3.93 us -> none  [the longest x1 1.43 us: on_device(): jnp.dot(amplitudes[0], first_factor[0], preferred_element_type=jnp.float32)]
  transfers between devices with their start and end apart: 1 -> 0, of which waited for: 1 -> 0; matrix products, arithmetic and copies ran while one was open for 1% -> 0% of each run, Pallas kernels for 0% -> 0%
where the time goes in v1:
time: 23.7 us; the launch traced here: 23.6 us
  Pallas kernels  22.9 us (97%)
  local copies, waits for them, and re-layouts  0.63 us (3%)
    pallas_call x1, Pallas kernels, on_device(): pl.pallas_call(kernel, out_shape=pltpu.VMEM((2, 2, JLO, M), BF16), in_spe...  22.9 us
    unnamed x1, local copies, waits for them, and re-layouts  0.63 us

profile of v1, /device:TPU:1, one launch (start us, length us, event | category | flops | bytes accessed | tf_op | source)
XLA Modules:
  0.0 23.6 jit_solution(8599432685867728719)
XLA Ops:
  0.0 22.9 %shard_map.37 = bf16[2,2,16,512]{3,2,1,0:T(8,128)(2,1)S(1)} custom-call(bf16[2,64,1024]{2,1,0:T(8,128)(2,1)} %bitcast.1, bf16[2,64,512]{2,1,0:T(8,128)(2,1)} %ff_ref.1, bf16[2,1024,512]{2,1,0:T(8,128)(2,1)} %sf_ref.1), custom_call_target="tpu_custom_call" | custom-call | flops 800000000 | bytes 2600000 | tf_op jit(solution)/shard_map/pallas_call | solution.py:206
  22.9 0.6 %copy.5 = bf16[2,2,16,512]{3,2,1,0:T(8,128)(2,1)} copy(bf16[2,2,16,512]{3,2,1,0:T(8,128)(2,1)S(1)} %shard_map.37) | data formatting | bytes 131072

commit v2 on v1

v2 whole, which is shorter than its diff:
```python
import jax
import jax.numpy as jnp
from jax import lax
from jax.experimental import pallas as pl
from jax.experimental.pallas import tpu as pltpu
from jax.sharding import PartitionSpec as P

MESH = pl.DeviceIdType.MESH
XS = 4
YS = 8
JHI = 32
RLO = 32
JLO = 16
J = JHI * JLO
G2 = RLO * JHI
M = 512
KH = 64
KB = 128
ROWS = 128
CHUNKS = 2
CJ = J // CHUNKS
F32 = jnp.float32
BF16 = jnp.bfloat16


def kernel(at_ref, ff_ref, sf_ref, out_ref,
           s_vmem, abuf, bbuf, rows_t, left, acc, half_send, half_recv, z_send, z_recv, lhs,
           local_sem, a_sems, x_sems, y_sems, half_sems, z_sems):
    grid = lax.axis_index("grid")
    depth = lax.axis_index("depth")
    x = depth // 4
    zl = (depth // 2) % 2
    core = depth % 2
    zh = grid // YS
    y = grid % YS

    def device(dx):
        return grid, (lax.rem(x + dx, XS) * 2 + zl) * 2 + (core if dx % 2 == 0 else 1 - core)

    xp, xm, x2 = device(1), device(3), device(2)
    yp = (zh * YS + lax.rem(y + 1, YS), depth)
    ym = (zh * YS + lax.rem(y + YS - 1, YS), depth)
    zp = (grid, (x * 2 + 1 - zl) * 2 + core)
    zc = (grid, (x * 2 + 1 - zl) * 2 + 1 - core)
    sibling = (grid, (x * 2 + zl) * 2 + 1 - core)
    partners = (xp, xm, yp, ym, x2, zp, zc, sibling)

    barrier = pltpu.get_barrier_semaphore()
    for partner in partners:
        pl.semaphore_signal(barrier, inc=1, device_id=partner, device_id_type=MESH)

    def rows_of(dx, z):
        return pl.ds(pl.multiple_of((lax.rem(x + dx, XS) * 2 + z) * ROWS, ROWS), ROWS)

    z_of = (1 - zl, zl)
    load_b = pltpu.make_async_copy(ff_ref, bbuf.at[0], local_sem.at[0])
    load_a = [pltpu.make_async_copy(at_ref.at[:, :, rows_of(0, z_of[s])], abuf.at[s, 0], local_sem.at[1 + s])
              for s in range(2)]
    load_s = pltpu.make_async_copy(sf_ref, s_vmem, local_sem.at[3])

    def remote(src, dst, sems, i, to):
        return pltpu.make_async_remote_copy(
            src_ref=src, dst_ref=dst, send_sem=sems.at[0, i], recv_sem=sems.at[1, i],
            device_id=to, device_id_type=MESH)

    up = y % 2
    down = 1 - up
    from_xm = remote(ff_ref.at[up], bbuf.at[1, up], x_sems, 0, xp)
    from_xp = remote(ff_ref.at[down], bbuf.at[3, down], x_sems, 1, xm)
    relay_p = remote(bbuf.at[1, up], bbuf.at[2, up], x_sems, 2, xp)
    relay_m = remote(bbuf.at[3, down], bbuf.at[2, down], x_sems, 3, xm)
    to_yp = remote(bbuf.at[1, up], bbuf.at[1, up], y_sems, 0, yp)
    to_ym = remote(bbuf.at[3, down], bbuf.at[3, down], y_sems, 1, ym)
    from_ym = remote(bbuf.at[1, down], bbuf.at[1, down], y_sems, 0, yp)
    from_yp = remote(bbuf.at[3, up], bbuf.at[3, up], y_sems, 1, ym)
    a_copies = [[remote(at_ref.at[:, :, rows_of(dx, z_of[s])], abuf.at[s, dx], a_sems, s * 3 + dx - 1, device(dx))
                 for dx in (1, 3, 2)] for s in range(2)]

    pl.semaphore_wait(barrier, len(partners))
    from_xm.start()
    from_xp.start()
    for copy in a_copies[0] + a_copies[1]:
        copy.start()
    load_b.start()
    load_a[0].start()
    load_a[1].start()

    minus = jnp.where(lax.broadcasted_iota(jnp.int32, (64, KB), 1) < KH, 1.0, -1.0)

    def weigh(s):
        load_a[s].wait()
        for copy in a_copies[s]:
            copy.wait_recv()

        @pl.loop(0, XS)
        def _(slot):
            rows_t[...] = abuf[s, slot].reshape(KB, ROWS).T.astype(F32)
            lanes = pl.ds(pl.multiple_of(slot * KB, KB), KB)
            for side in range(2):
                which = core if side == 0 else 1 - core
                value = rows_t[pl.ds(pl.multiple_of(which * 64, 64), 64)]
                left[s, pl.ds(side * 128, 64), lanes] = (value * minus).astype(BF16)
                left[s, pl.ds(side * 128 + 64, 64), lanes] = pltpu.roll(value, KH, 1).astype(BF16)

    half_copies = {(s, chunk): remote(half_send.at[s, chunk], half_recv.at[s, chunk], half_sems, 2 * s + chunk, sibling)
                   for s, chunk in ((0, 0), (1, 0), (1, 1))}
    z_copies = [[remote(z_send.at[0, 0], z_recv.at[0, 0], z_sems, 0, zp)],
                [remote(z_send.at[i, 1], z_recv.at[i, 1], z_sems, 1 + i, (zp, zc)[i]) for i in range(2)]]

    def contract(s, chunk):
        where = pl.ds(chunk * CJ, CJ)
        right = jnp.concatenate([bbuf[slot, :, :, where].reshape(KB, CJ) for slot in range(XS)], axis=0)
        return jnp.dot(left[s], right, preferred_element_type=F32)

    def halve(s, chunk):
        total = contract(s, chunk)
        acc[s, chunk] = total[:128]
        half_send[s, chunk] = total[128:].astype(BF16)
        half_copies[s, chunk].start()

    from_xm.wait_recv()
    relay_p.start()
    to_yp.start()
    from_xp.wait_recv()
    relay_m.start()
    to_ym.start()
    load_s.start()
    weigh(0)
    load_b.wait()
    for copy in (relay_p, relay_m, from_ym, from_yp):
        copy.wait_recv()
    halve(0, 0)
    total = contract(0, 1)
    z_send[0, 1] = total[:128].astype(BF16)
    z_copies[1][0].start()
    z_send[1, 1] = total[128:].astype(BF16)
    z_copies[1][1].start()
    half_copies[0, 0].wait_recv()
    z_send[0, 0] = (acc[0, 0] + half_recv[0, 0].astype(F32)).astype(BF16)
    z_copies[0][0].start()
    weigh(1)
    halve(1, 1)
    halve(1, 0)
    for copy in [from_xm, from_xp, relay_p, relay_m, to_yp, to_ym] + a_copies[0] + a_copies[1] + list(half_copies.values()):
        copy.wait_send()

    def swap(v, tile_bit, lane_bit):
        step, width = 1 << tile_bit, 1 << lane_bit
        v = v.reshape(16 // (2 * step), 2, step, JLO, 128)
        a = v[:, 0].reshape(8, JLO, 128)
        b = v[:, 1].reshape(8, JLO, 128)
        low = (lax.broadcasted_iota(jnp.int32, a.shape, 2) // width) % 2 == 0
        a, b = (jnp.where(low, a, pltpu.roll(b, width, 2)), jnp.where(low, pltpu.roll(a, 128 - width, 2), b))
        shape = (16 // (2 * step), 1, step, JLO, 128)
        return jnp.concatenate([a.reshape(shape), b.reshape(shape)], axis=1).reshape(16, JLO, 128)

    load_s.wait()

    result = jnp.zeros((64, M), F32)
    for top in (1, 0):
        half_copies[1, top].wait_recv()
        for copy in z_copies[top]:
            copy.wait_recv()
        total = acc[1, top] + half_recv[1, top].astype(F32) + z_recv[0, top].astype(F32)
        if top == 1:
            total += z_recv[1, top].astype(F32)
        value = total.astype(BF16).T.reshape(16, JLO, 128)
        for tile_bit, lane_bit in ((0, 0), (1, 1), (2, 2), (3, 3), (3, 6), (2, 5)):
            value = swap(value, tile_bit, lane_bit)
        right = []
        for u in range(4):
            for p in range(2):
                at = pl.ds((u * 2 + p) * 128, 128)
                turned = pl.ds((u * 2 + 1 - p) * 128, 128)
                for rh in range(2):
                    block = value[p * 8 + rh * 4 + u]
                    lhs[top, pl.ds(rh * 16, 16), at] = block if p == 0 else -block
                    lhs[top, pl.ds(32 + rh * 16, 16), turned] = block
                for t in range(8):
                    rl = (t % 2) * 16 + (t // 4) * 8 + (t // 2 % 2) * 4 + u
                    right.append(s_vmem[p, pl.ds(rl * JHI + top * 16, 16)])
        result += jnp.dot(lhs[top], jnp.concatenate(right, axis=0), preferred_element_type=F32)
    out_ref[...] = result.astype(BF16).reshape(2, 2, JLO, M)

    for copy in z_copies[0] + z_copies[1]:
        copy.wait_send()


def on_device(amplitudes, first_factor, second_factor):
    arguments = [pltpu.with_memory_space_constraint(a, pltpu.HBM)
                 for a in (jnp.swapaxes(amplitudes, 1, 2), first_factor, second_factor)]
    return pl.pallas_call(
        kernel,
        out_shape=pltpu.VMEM((2, 2, JLO, M), BF16),
        in_specs=[pl.BlockSpec(memory_space=pltpu.HBM)] * 3,
        out_specs=pl.BlockSpec(memory_space=pltpu.VMEM),
        scratch_shapes=[
            pltpu.VMEM((2, G2, M), BF16),
            pltpu.VMEM((2, XS, 2, KH, ROWS), BF16),
            pltpu.VMEM((XS, 2, KH, J), BF16),
            pltpu.VMEM((ROWS, KB), F32),
            pltpu.VMEM((2, 256, XS * KB), BF16),
            pltpu.VMEM((2, CHUNKS, 128, CJ), F32),
            pltpu.VMEM((2, CHUNKS, 128, CJ), BF16),
            pltpu.VMEM((2, CHUNKS, 128, CJ), BF16),
            pltpu.VMEM((2, CHUNKS, 128, CJ), BF16),
            pltpu.VMEM((2, CHUNKS, 128, CJ), BF16),
            pltpu.VMEM((2, 64, G2), BF16),
            pltpu.SemaphoreType.DMA((4,)),
            pltpu.SemaphoreType.DMA((2, 6)),
            pltpu.SemaphoreType.DMA((2, 4)),
            pltpu.SemaphoreType.DMA((2, 2)),
            pltpu.SemaphoreType.DMA((2, 2 * CHUNKS)),
            pltpu.SemaphoreType.DMA((2, 3)),
        ],
        compiler_params=pltpu.CompilerParams(
            collective_id=0, has_side_effects=True, vmem_limit_bytes=32 * 1024 * 1024),
        cost_estimate=pl.CostEstimate(flops=800_000_000, bytes_accessed=2_600_000, transcendentals=0),
    )(*arguments)


def solution(mesh):
    return jax.shard_map(
        on_device, mesh=mesh,
        in_specs=(P(None, "grid", "depth"), P(None, "depth", None), P()),
        out_specs=P(None, ("grid", "depth"), None, None), check_vma=False)
```

time: 23.7 us -> 23.6 us (level)
  no operation moved by 1% of the time
where the time goes in v2:
time: 23.6 us; the launch traced here: 23.5 us
  Pallas kernels  22.8 us (97%)
  local copies, waits for them, and re-layouts  0.63 us (3%)
    pallas_call x1, Pallas kernels, on_device(): pl.pallas_call(kernel, out_shape=pltpu.VMEM((2, 2, JLO, M), BF16), in_spe...  22.8 us
    unnamed x1, local copies, waits for them, and re-layouts  0.63 us

profile of v2, /device:TPU:1, one launch (start us, length us, event | category | flops | bytes accessed | tf_op | source)
XLA Modules:
  0.0 23.5 jit_solution(4390062683291105326)
XLA Ops:
  0.0 22.8 %shard_map.37 = bf16[2,2,16,512]{3,2,1,0:T(8,128)(2,1)S(1)} custom-call(bf16[2,64,1024]{2,1,0:T(8,128)(2,1)} %bitcast.1, bf16[2,64,512]{2,1,0:T(8,128)(2,1)} %ff_ref.1, bf16[2,1024,512]{2,1,0:T(8,128)(2,1)} %sf_ref.1), custom_call_target="tpu_custom_call" | custom-call | flops 800000000 | bytes 2600000 | tf_op jit(solution)/shard_map/pallas_call | solution.py:192
  22.8 0.6 %copy.5 = bf16[2,2,16,512]{3,2,1,0:T(8,128)(2,1)} copy(bf16[2,2,16,512]{3,2,1,0:T(8,128)(2,1)S(1)} %shard_map.37) | data formatting | bytes 131072

commit v3 on v2

--- a/solution.py
+++ b/solution.py
@@ -79,7 +79,7 @@
     pl.semaphore_wait(barrier, len(partners))
     from_xm.start()
     from_xp.start()
-    for copy in a_copies[0] + a_copies[1]:
+    for copy in a_copies[0]:
         copy.start()
     load_b.start()
     load_a[0].start()
@@ -124,7 +124,8 @@
     from_xp.wait_recv()
     relay_m.start()
     to_ym.start()
-    load_s.start()
+    for copy in a_copies[1]:
+        copy.start()
     weigh(0)
     load_b.wait()
     for copy in (relay_p, relay_m, from_ym, from_yp):
@@ -138,6 +139,7 @@
     half_copies[0, 0].wait_recv()
     z_send[0, 0] = (acc[0, 0] + half_recv[0, 0].astype(F32)).astype(BF16)
     z_copies[0][0].start()
+    load_s.start()
     weigh(1)
     halve(1, 1)
     halve(1, 0)

time: 23.6 us -> 23.6 us (level)
  no operation moved by 1% of the time
where the time goes in v3:
time: 23.6 us; the launch traced here: 23.5 us
  Pallas kernels  22.8 us (97%)
  local copies, waits for them, and re-layouts  0.63 us (3%)
    pallas_call x1, Pallas kernels, on_device(): pl.pallas_call(kernel, out_shape=pltpu.VMEM((2, 2, JLO, M), BF16), in_spe...  22.8 us
    unnamed x1, local copies, waits for them, and re-layouts  0.63 us

profile of v3, /device:TPU:1, one launch (start us, length us, event | category | flops | bytes accessed | tf_op | source)
XLA Modules:
  0.0 23.5 jit_solution(1767729457954283055)
XLA Ops:
  0.0 22.8 %shard_map.37 = bf16[2,2,16,512]{3,2,1,0:T(8,128)(2,1)S(1)} custom-call(bf16[2,64,1024]{2,1,0:T(8,128)(2,1)} %bitcast.1, bf16[2,64,512]{2,1,0:T(8,128)(2,1)} %ff_ref.1, bf16[2,1024,512]{2,1,0:T(8,128)(2,1)} %sf_ref.1), custom_call_target="tpu_custom_call" | custom-call | flops 800000000 | bytes 2600000 | tf_op jit(solution)/shard_map/pallas_call | solution.py:194
  22.8 0.6 %copy.5 = bf16[2,2,16,512]{3,2,1,0:T(8,128)(2,1)} copy(bf16[2,2,16,512]{3,2,1,0:T(8,128)(2,1)S(1)} %shard_map.37) | data formatting | bytes 131072

commit v4 on v0

v4 whole, which is shorter than its diff:
```python
import jax
import jax.numpy as jnp
from jax import lax
from jax.experimental import pallas as pl
from jax.experimental.pallas import tpu as pltpu
from jax.sharding import PartitionSpec as P

MESH = pl.DeviceIdType.MESH
XS = 4
JHI = 32
RLO = 32
JLO = 16
J = JHI * JLO
G2 = RLO * JHI
M = 512
KH = 64
KB = 128
ROWS = 128
CHUNKS = 2
CJ = J // CHUNKS
F32 = jnp.float32
BF16 = jnp.bfloat16


def kernel(at_ref, ff_ref, sf_ref, out_ref,
           s_vmem, abuf, bbuf, left, own_send, own_part, z_send, z_recv, lhs,
           local_sem, ready, b_send, b_recv, a_send, a_recv, r_sems, own_sems, z_out, z_in):
    grid = lax.axis_index("grid")
    depth = lax.axis_index("depth")
    x = depth // 4
    zl = (depth // 2) % 2
    core = depth % 2

    def device(dx, which):
        return grid, (lax.rem(x + dx, XS) * 2 + zl) * 2 + which

    def z_device(which):
        return grid, (x * 2 + 1 - zl) * 2 + which

    def rows_of(dx, z):
        return pl.ds(pl.multiple_of((lax.rem(x + dx, XS) * 2 + z) * ROWS, ROWS), ROWS)

    def remote(src, dst, send, recv, to):
        return pltpu.make_async_remote_copy(
            src_ref=src, dst_ref=dst, send_sem=send, recv_sem=recv, device_id=to, device_id_type=MESH)

    z_of = (1 - zl, zl)
    load_s = pltpu.make_async_copy(sf_ref, s_vmem, local_sem.at[3])
    barrier = pltpu.get_barrier_semaphore()

    def b_copy(c, dx, p):
        i = (0 if dx == 1 else 2) + p
        return remote(ff_ref.at[p], bbuf.at[c, dx, p], b_send.at[i], b_recv.at[c * 4 + i], device(dx, 1))

    def a_copy(c, s, dx):
        i = s * 3 + dx - 1
        return remote(at_ref.at[:, :, rows_of(dx, z_of[s])], abuf.at[s, c, dx], a_send.at[i], a_recv.at[c * 6 + i], device(dx, 1))

    b_own = remote(ff_ref, bbuf.at[0, 0], b_send.at[4], b_recv.at[8], device(0, 1))
    a_own = [remote(at_ref.at[:, :, rows_of(0, z_of[s])], abuf.at[s, 0, 0], a_send.at[6 + s], a_recv.at[12 + s], device(0, 1))
             for s in range(2)]
    own_copies = [remote(own_send.at[h], own_part.at[h], own_sems.at[0, h], own_sems.at[1, h], device(0, 0)) for h in range(2)]
    z_copies = [[remote(z_send.at[c, h], z_recv.at[h], z_out.at[2 * h + c], z_in.at[h], z_device(c)) for c in range(2)]
                for h in range(2)]

    @pl.when(core == 0)
    def _():
        pl.semaphore_wait(barrier, 5)
        for dx, p in ((1, 0), (3, 1)):
            b_copy(0, dx, p).start()
        for dx in (1, 3, 2):
            a_copy(0, 0, dx).start()
        b_own.start()
        for dx, p in ((1, 1), (3, 0)):
            b_copy(0, dx, p).start()
        a_own[0].start()
        for dx in (1, 3, 2):
            a_copy(0, 1, dx).start()
        a_own[1].start()
        for to in (device(0, 1), z_device(1)):
            pl.semaphore_signal(ready, inc=1, device_id=to, device_id_type=MESH)
        load_s.start()
        for dx in (1, 3):
            for p in range(2):
                b_copy(0, dx, p).wait_send()
        for s in range(2):
            for dx in (1, 3, 2):
                a_copy(0, s, dx).wait_send()
            a_own[s].wait_send()
        b_own.wait_send()

    minus = jnp.where(lax.broadcasted_iota(jnp.int32, (64, KB), 1) < KH, 1.0, -1.0)

    def weigh(s, c, slot):
        turned = abuf[s, c, slot].reshape(KB, ROWS).T.astype(F32)
        lanes = pl.ds((c * XS + slot) * KB, KB)
        for side in range(2):
            value = turned[side * 64:(side + 1) * 64]
            left[s, pl.ds(side * 128, 64), lanes] = (value * minus).astype(BF16)
            left[s, pl.ds(side * 128 + 64, 64), lanes] = pltpu.roll(value, KH, 1).astype(BF16)

    def contract(s, h):
        where = pl.ds(h * CJ, CJ)
        right = jnp.concatenate([bbuf[c, slot, :, :, where].reshape(KB, CJ) for c in range(2) for slot in range(XS)], axis=0)
        return jnp.dot(left[s], right, preferred_element_type=F32)

    @pl.when(core == 1)
    def _():
        for to in [device(dx, 1) for dx in (1, 3, 2)] + [z_device(1)]:
            pl.semaphore_signal(barrier, inc=1, device_id=to, device_id_type=MESH)
        for to in [device(dx, 0) for dx in range(XS)] + [z_device(0)]:
            pl.semaphore_signal(barrier, inc=1, device_id=to, device_id_type=MESH)
        load_b = pltpu.make_async_copy(ff_ref, bbuf.at[1, 0], local_sem.at[0])
        load_a = [pltpu.make_async_copy(at_ref.at[:, :, rows_of(0, z_of[s])], abuf.at[s, 1, 0], local_sem.at[1 + s])
                  for s in range(2)]
        relays = [(remote(bbuf.at[c, 1, 0], bbuf.at[c, 2, 0], r_sems.at[0, 2 * c], r_sems.at[1, 2 * c], device(1, 1)),
                   remote(bbuf.at[c, 3, 1], bbuf.at[c, 2, 1], r_sems.at[0, 2 * c + 1], r_sems.at[1, 2 * c + 1], device(3, 1)))
                  for c in range(2)]

        pl.semaphore_wait(barrier, 4)
        for dx, p in ((1, 0), (3, 1)):
            b_copy(1, dx, p).start()
        for dx in (1, 3, 2):
            a_copy(1, 0, dx).start()
        for dx, p in ((1, 1), (3, 0)):
            b_copy(1, dx, p).start()
        load_b.start()
        load_a[0].start()
        load_a[1].start()
        for c in (1, 0):
            b_copy(c, 1, 0).wait_recv()
            relays[c][0].start()
            b_copy(c, 3, 1).wait_recv()
            relays[c][1].start()
        for dx in (1, 3, 2):
            a_copy(1, 1, dx).start()
        load_s.start()
        load_a[0].wait()
        weigh(0, 1, 0)
        for c in (1, 0):
            for dx in (1, 3, 2):
                a_copy(c, 0, dx).wait_recv()
                weigh(0, c, dx)
        a_own[0].wait_recv()
        weigh(0, 0, 0)
        load_b.wait()
        b_own.wait_recv()
        for c in (1, 0):
            b_copy(c, 1, 1).wait_recv()
            b_copy(c, 3, 0).wait_recv()
        for c in (1, 0):
            relays[c][0].wait_recv()
            relays[c][1].wait_recv()
        pl.semaphore_wait(ready, 2)
        for h in range(2):
            total = contract(0, h)
            for c in range(2):
                z_send[c, h] = total[c * 128:(c + 1) * 128].astype(BF16)
                z_copies[h][c].start()
        load_a[1].wait()
        weigh(1, 1, 0)
        for c in (1, 0):
            for dx in (1, 3, 2):
                a_copy(c, 1, dx).wait_recv()
                weigh(1, c, dx)
        a_own[1].wait_recv()
        weigh(1, 0, 0)
        for h in range(2):
            total = contract(1, h)
            own_send[h] = total[:128].astype(BF16)
            own_copies[h].start()
            own_part[h] = total[128:].astype(BF16)
        for dx in (1, 3):
            for p in range(2):
                b_copy(1, dx, p).wait_send()
        for s in range(2):
            for dx in (1, 3, 2):
                a_copy(1, s, dx).wait_send()
        for c in range(2):
            relays[c][0].wait_send()
            relays[c][1].wait_send()

    def swap(v, tile_bit, lane_bit):
        step, width = 1 << tile_bit, 1 << lane_bit
        v = v.reshape(16 // (2 * step), 2, step, JLO, 128)
        a = v[:, 0].reshape(8, JLO, 128)
        b = v[:, 1].reshape(8, JLO, 128)
        low = (lax.broadcasted_iota(jnp.int32, a.shape, 2) // width) % 2 == 0
        a, b = (jnp.where(low, a, pltpu.roll(b, width, 2)), jnp.where(low, pltpu.roll(a, 128 - width, 2), b))
        shape = (16 // (2 * step), 1, step, JLO, 128)
        return jnp.concatenate([a.reshape(shape), b.reshape(shape)], axis=1).reshape(16, JLO, 128)

    load_s.wait()

    result = jnp.zeros((64, M), F32)
    for top in range(2):
        @pl.when(core == 0)
        def _(top=top):
            own_copies[top].wait_recv()

        z_copies[top][0].wait_recv()
        total = own_part[top].astype(F32) + z_recv[top].astype(F32)
        value = total.astype(BF16).T.reshape(16, JLO, 128)
        for tile_bit, lane_bit in ((0, 0), (1, 1), (2, 2), (3, 3), (3, 6), (2, 5)):
            value = swap(value, tile_bit, lane_bit)
        right = []
        for u in range(4):
            for p in range(2):
                at = pl.ds((u * 2 + p) * 128, 128)
                turned = pl.ds((u * 2 + 1 - p) * 128, 128)
                for rh in range(2):
                    block = value[p * 8 + rh * 4 + u]
                    lhs[top, pl.ds(rh * 16, 16), at] = block if p == 0 else -block
                    lhs[top, pl.ds(32 + rh * 16, 16), turned] = block
                for t in range(8):
                    rl = (t % 2) * 16 + (t // 4) * 8 + (t // 2 % 2) * 4 + u
                    right.append(s_vmem[p, pl.ds(rl * JHI + top * 16, 16)])
        result += jnp.dot(lhs[top], jnp.concatenate(right, axis=0), preferred_element_type=F32)
    out_ref[...] = result.astype(BF16).reshape(2, 2, JLO, M)

    @pl.when(core == 1)
    def _():
        for copy in own_copies + z_copies[0] + z_copies[1]:
            copy.wait_send()


def on_device(amplitudes, first_factor, second_factor):
    arguments = [pltpu.with_memory_space_constraint(a, pltpu.HBM)
                 for a in (jnp.swapaxes(amplitudes, 1, 2), first_factor, second_factor)]
    return pl.pallas_call(
        kernel,
        out_shape=pltpu.VMEM((2, 2, JLO, M), BF16),
        in_specs=[pl.BlockSpec(memory_space=pltpu.HBM)] * 3,
        out_specs=pl.BlockSpec(memory_space=pltpu.VMEM),
        scratch_shapes=[
            pltpu.VMEM((2, G2, M), BF16),
            pltpu.VMEM((2, 2, XS, 2, KH, ROWS), BF16),
            pltpu.VMEM((2, XS, 2, KH, J), BF16),
            pltpu.VMEM((2, 256, 2 * XS * KB), BF16),
            pltpu.VMEM((CHUNKS, 128, CJ), BF16),
            pltpu.VMEM((CHUNKS, 128, CJ), BF16),
            pltpu.VMEM((2, CHUNKS, 128, CJ), BF16),
            pltpu.VMEM((CHUNKS, 128, CJ), BF16),
            pltpu.VMEM((2, 64, G2), BF16),
            pltpu.SemaphoreType.DMA((4,)),
            pltpu.SemaphoreType.REGULAR,
            pltpu.SemaphoreType.DMA((5,)),
            pltpu.SemaphoreType.DMA((9,)),
            pltpu.SemaphoreType.DMA((8,)),
            pltpu.SemaphoreType.DMA((14,)),
            pltpu.SemaphoreType.DMA((2, 4)),
            pltpu.SemaphoreType.DMA((2, 2)),
            pltpu.SemaphoreType.DMA((4,)),
            pltpu.SemaphoreType.DMA((2,)),
        ],
        compiler_params=pltpu.CompilerParams(
            collective_id=0, has_side_effects=True, vmem_limit_bytes=32 * 1024 * 1024),
        cost_estimate=pl.CostEstimate(flops=800_000_000, bytes_accessed=2_600_000, transcendentals=0),
    )(*arguments)


def solution(mesh):
    return jax.shard_map(
        on_device, mesh=mesh,
        in_specs=(P(None, "grid", "depth"), P(None, "depth", None), P()),
        out_specs=P(None, ("grid", "depth"), None, None), check_vma=False)
```

time: 187 us -> 21.2 us (0.11)
  waiting for transfers between devices: 138 us -> 0 us
  blocking collectives: 20.8 us -> 0 us
  Pallas kernels: 0 us -> 20.4 us
  between operations: 14.1 us -> 0.01 us
  local copies, waits for them, and re-layouts: 8.92 us -> 0.63 us
  matrix products: 3.93 us -> 0 us
    unnamed x2 -> x0, waiting for transfers between devices: 138 us -> none
    all_to_all x2 -> x0, blocking collectives: 20.8 us -> none  [the longest x1 11.8 us: on_device(): lax.all_to_all(contracted, 'depth', split_axis=3, concat_axis=2, tiled=True)]
    pallas_call x0 -> x1, Pallas kernels: none -> 20.4 us  [on_device(): pl.pallas_call(kernel, out_shape=pltpu.VMEM((2, 2, JLO, M), BF16), in_spe...]
    another operation x2 -> x0, local copies, waits for them, and re-layouts: 4.09 us -> none  [the longest x1 4.02 us: on_device(): terms = jnp.stack((real_part, imag_part), axis=1)]
    dot_general x8 -> x0, matrix products: 3.93 us -> none  [the longest x1 1.43 us: on_device(): jnp.dot(amplitudes[0], first_factor[0], preferred_element_type=jnp.float32)]
  transfers between devices with their start and end apart: 1 -> 0, of which waited for: 1 -> 0; matrix products, arithmetic and copies ran while one was open for 1% -> 0% of each run, Pallas kernels for 0% -> 0%
where the time goes in v4:
time: 21.2 us; the launch traced here: 21.1 us
  Pallas kernels  20.4 us (96%)
  local copies, waits for them, and re-layouts  0.63 us (3%)
    pallas_call x1, Pallas kernels, on_device(): pl.pallas_call(kernel, out_shape=pltpu.VMEM((2, 2, JLO, M), BF16), in_spe...  20.4 us
    unnamed x1, local copies, waits for them, and re-layouts  0.63 us

profile of v4, /device:TPU:1, one launch (start us, length us, event | category | flops | bytes accessed | tf_op | source)
XLA Modules:
  0.0 21.1 jit_solution(6837507275005219017)
XLA Ops:
  0.0 20.4 %shard_map.37 = bf16[2,2,16,512]{3,2,1,0:T(8,128)(2,1)S(1)} custom-call(bf16[2,64,1024]{2,1,0:T(8,128)(2,1)} %bitcast.1, bf16[2,64,512]{2,1,0:T(8,128)(2,1)} %ff_ref.1, bf16[2,1024,512]{2,1,0:T(8,128)(2,1)} %sf_ref.1), custom_call_target="tpu_custom_call" | custom-call | flops 800000000 | bytes 2600000 | tf_op jit(solution)/shard_map/pallas_call | solution.py:230
  20.4 0.6 %copy.5 = bf16[2,2,16,512]{3,2,1,0:T(8,128)(2,1)} copy(bf16[2,2,16,512]{3,2,1,0:T(8,128)(2,1)S(1)} %shard_map.37) | data formatting | bytes 131072

commit v5 on v4

--- a/solution.py
+++ b/solution.py
@@ -23,7 +23,7 @@
 
 
 def kernel(at_ref, ff_ref, sf_ref, out_ref,
-           s_vmem, abuf, bbuf, left, own_send, own_part, z_send, z_recv, lhs,
+           s_vmem, abuf, bbuf, left, acc, own_send, own_part, z_send, z_recv, lhs,
            local_sem, ready, b_send, b_recv, a_send, a_recv, r_sems, own_sems, z_out, z_in):
     grid = lax.axis_index("grid")
     depth = lax.axis_index("depth")
@@ -89,20 +89,22 @@
             a_own[s].wait_send()
         b_own.wait_send()
 
-    minus = jnp.where(lax.broadcasted_iota(jnp.int32, (64, KB), 1) < KH, 1.0, -1.0)
+    minus = jnp.where(lax.broadcasted_iota(jnp.int32, (64, KB), 1) < KH, 1.0, -1.0).astype(BF16)
+
+    order = [(c, slot) for slot in (0, 1, 3, 2) for c in range(2)]
 
     def weigh(s, c, slot):
-        turned = abuf[s, c, slot].reshape(KB, ROWS).T.astype(F32)
-        lanes = pl.ds((c * XS + slot) * KB, KB)
+        turned = abuf[s, c, slot].reshape(KB, ROWS).T
+        lanes = pl.ds(order.index((c, slot)) * KB, KB)
         for side in range(2):
             value = turned[side * 64:(side + 1) * 64]
-            left[s, pl.ds(side * 128, 64), lanes] = (value * minus).astype(BF16)
-            left[s, pl.ds(side * 128 + 64, 64), lanes] = pltpu.roll(value, KH, 1).astype(BF16)
-
-    def contract(s, h):
+            left[s, pl.ds(side * 128, 64), lanes] = value * minus
+            left[s, pl.ds(side * 128 + 64, 64), lanes] = pltpu.roll(value, KH, 1)
+
+    def contract(s, h, first, last):
         where = pl.ds(h * CJ, CJ)
-        right = jnp.concatenate([bbuf[c, slot, :, :, where].reshape(KB, CJ) for c in range(2) for slot in range(XS)], axis=0)
-        return jnp.dot(left[s], right, preferred_element_type=F32)
+        right = jnp.concatenate([bbuf[c, slot, :, :, where].reshape(KB, CJ) for c, slot in order[first:last]], axis=0)
+        return jnp.dot(left[s, :, pl.ds(first * KB, (last - first) * KB)], right, preferred_element_type=F32)
 
     @pl.when(core == 1)
     def _():
@@ -138,7 +140,7 @@
         load_a[0].wait()
         weigh(0, 1, 0)
         for c in (1, 0):
-            for dx in (1, 3, 2):
+            for dx in (1, 3):
                 a_copy(c, 0, dx).wait_recv()
                 weigh(0, c, dx)
         a_own[0].wait_recv()
@@ -148,12 +150,17 @@
         for c in (1, 0):
             b_copy(c, 1, 1).wait_recv()
             b_copy(c, 3, 0).wait_recv()
+        for h in range(2):
+            acc[h] = contract(0, h, 0, 6)
+        for c in (1, 0):
+            a_copy(c, 0, 2).wait_recv()
+            weigh(0, c, 2)
         for c in (1, 0):
             relays[c][0].wait_recv()
             relays[c][1].wait_recv()
         pl.semaphore_wait(ready, 2)
         for h in range(2):
-            total = contract(0, h)
+            total = acc[h] + contract(0, h, 6, 8)
             for c in range(2):
                 z_send[c, h] = total[c * 128:(c + 1) * 128].astype(BF16)
                 z_copies[h][c].start()
@@ -166,7 +173,7 @@
         a_own[1].wait_recv()
         weigh(1, 0, 0)
         for h in range(2):
-            total = contract(1, h)
+            total = contract(1, h, 0, 8)
             own_send[h] = total[:128].astype(BF16)
             own_copies[h].start()
             own_part[h] = total[128:].astype(BF16)
@@ -237,6 +244,7 @@
             pltpu.VMEM((2, 2, XS, 2, KH, ROWS), BF16),
             pltpu.VMEM((2, XS, 2, KH, J), BF16),
             pltpu.VMEM((2, 256, 2 * XS * KB), BF16),
+            pltpu.VMEM((CHUNKS, 256, CJ), F32),
             pltpu.VMEM((CHUNKS, 128, CJ), BF16),
             pltpu.VMEM((CHUNKS, 128, CJ), BF16),
             pltpu.VMEM((2, CHUNKS, 128, CJ), BF16),

time: 21.2 us -> 21 us (level)
  no operation moved by 1% of the time
where the time goes in v5:
time: 21 us; the launch traced here: 20.9 us
  Pallas kernels  20.2 us (96%)
  local copies, waits for them, and re-layouts  0.63 us (3%)
    pallas_call x1, Pallas kernels, on_device(): pl.pallas_call(kernel, out_shape=pltpu.VMEM((2, 2, JLO, M), BF16), in_spe...  20.2 us
    unnamed x1, local copies, waits for them, and re-layouts  0.63 us

profile of v5, /device:TPU:1, one launch (start us, length us, event | category | flops | bytes accessed | tf_op | source)
XLA Modules:
  0.0 20.9 jit_solution(17089072602239225851)
XLA Ops:
  0.0 20.2 %shard_map.37 = bf16[2,2,16,512]{3,2,1,0:T(8,128)(2,1)S(1)} custom-call(bf16[2,64,1024]{2,1,0:T(8,128)(2,1)} %bitcast.1, bf16[2,64,512]{2,1,0:T(8,128)(2,1)} %ff_ref.1, bf16[2,1024,512]{2,1,0:T(8,128)(2,1)} %sf_ref.1), custom_call_target="tpu_custom_call" | custom-call | flops 800000000 | bytes 2600000 | tf_op jit(solution)/shard_map/pallas_call | solution.py:237
  20.2 0.6 %copy.5 = bf16[2,2,16,512]{3,2,1,0:T(8,128)(2,1)} copy(bf16[2,2,16,512]{3,2,1,0:T(8,128)(2,1)S(1)} %shard_map.37) | data formatting | bytes 131072

commit v6 on v5

--- a/solution.py
+++ b/solution.py
@@ -68,17 +68,17 @@
         pl.semaphore_wait(barrier, 5)
         for dx, p in ((1, 0), (3, 1)):
             b_copy(0, dx, p).start()
+        for to in (device(0, 1), z_device(1)):
+            pl.semaphore_signal(ready, inc=1, device_id=to, device_id_type=MESH)
         for dx in (1, 3, 2):
             a_copy(0, 0, dx).start()
-        b_own.start()
         for dx, p in ((1, 1), (3, 0)):
             b_copy(0, dx, p).start()
+        b_own.start()
         a_own[0].start()
+        a_own[1].start()
         for dx in (1, 3, 2):
             a_copy(0, 1, dx).start()
-        a_own[1].start()
-        for to in (device(0, 1), z_device(1)):
-            pl.semaphore_signal(ready, inc=1, device_id=to, device_id_type=MESH)
         load_s.start()
         for dx in (1, 3):
             for p in range(2):

time: 21 us -> 21 us (level)
  no operation moved by 1% of the time
where the time goes in v6:
time: 21 us; the launch traced here: 20.9 us
  Pallas kernels  20.2 us (96%)
  local copies, waits for them, and re-layouts  0.63 us (3%)
    pallas_call x1, Pallas kernels, on_device(): pl.pallas_call(kernel, out_shape=pltpu.VMEM((2, 2, JLO, M), BF16), in_spe...  20.2 us
    unnamed x1, local copies, waits for them, and re-layouts  0.63 us

profile of v6, /device:TPU:1, one launch (start us, length us, event | category | flops | bytes accessed | tf_op | source)
XLA Modules:
  0.0 20.9 jit_solution(6138257503845095588)
XLA Ops:
  0.0 20.2 %shard_map.37 = bf16[2,2,16,512]{3,2,1,0:T(8,128)(2,1)S(1)} custom-call(bf16[2,64,1024]{2,1,0:T(8,128)(2,1)} %bitcast.1, bf16[2,64,512]{2,1,0:T(8,128)(2,1)} %ff_ref.1, bf16[2,1024,512]{2,1,0:T(8,128)(2,1)} %sf_ref.1), custom_call_target="tpu_custom_call" | custom-call | flops 800000000 | bytes 2600000 | tf_op jit(solution)/shard_map/pallas_call | solution.py:237
  20.2 0.6 %copy.5 = bf16[2,2,16,512]{3,2,1,0:T(8,128)(2,1)} copy(bf16[2,2,16,512]{3,2,1,0:T(8,128)(2,1)S(1)} %shard_map.37) | data formatting | bytes 131072

commit v7 on v6

--- a/solution.py
+++ b/solution.py
@@ -166,14 +166,19 @@
                 z_copies[h][c].start()
         load_a[1].wait()
         weigh(1, 1, 0)
-        for c in (1, 0):
-            for dx in (1, 3, 2):
+        a_own[1].wait_recv()
+        weigh(1, 0, 0)
+        for c in (1, 0):
+            for dx in (1, 3):
                 a_copy(c, 1, dx).wait_recv()
                 weigh(1, c, dx)
-        a_own[1].wait_recv()
-        weigh(1, 0, 0)
-        for h in range(2):
-            total = contract(1, h, 0, 8)
+        for h in range(2):
+            acc[h] = contract(1, h, 0, 6)
+        for c in (1, 0):
+            a_copy(c, 1, 2).wait_recv()
+            weigh(1, c, 2)
+        for h in range(2):
+            total = acc[h] + contract(1, h, 6, 8)
             own_send[h] = total[:128].astype(BF16)
             own_copies[h].start()
             own_part[h] = total[128:].astype(BF16)

time: 21 us -> 21 us (level)
  no operation moved by 1% of the time
where the time goes in v7:
time: 21 us; the launch traced here: 20.9 us
  Pallas kernels  20.2 us (96%)
  local copies, waits for them, and re-layouts  0.63 us (3%)
    pallas_call x1, Pallas kernels, on_device(): pl.pallas_call(kernel, out_shape=pltpu.VMEM((2, 2, JLO, M), BF16), in_spe...  20.2 us
    unnamed x1, local copies, waits for them, and re-layouts  0.63 us

profile of v7, /device:TPU:1, one launch (start us, length us, event | category | flops | bytes accessed | tf_op | source)
XLA Modules:
  0.0 20.9 jit_solution(5833710312090172047)
XLA Ops:
  0.0 20.2 %shard_map.37 = bf16[2,2,16,512]{3,2,1,0:T(8,128)(2,1)S(1)} custom-call(bf16[2,64,1024]{2,1,0:T(8,128)(2,1)} %bitcast.1, bf16[2,64,512]{2,1,0:T(8,128)(2,1)} %ff_ref.1, bf16[2,1024,512]{2,1,0:T(8,128)(2,1)} %sf_ref.1), custom_call_target="tpu_custom_call" | custom-call | flops 800000000 | bytes 2600000 | tf_op jit(solution)/shard_map/pallas_call | solution.py:242
  20.2 0.6 %copy.5 = bf16[2,2,16,512]{3,2,1,0:T(8,128)(2,1)} copy(bf16[2,2,16,512]{3,2,1,0:T(8,128)(2,1)S(1)} %shard_map.37) | data formatting | bytes 131072

commit v8 on v7

--- a/solution.py
+++ b/solution.py
@@ -7,6 +7,7 @@
 
 MESH = pl.DeviceIdType.MESH
 XS = 4
+LATE = 2
 JHI = 32
 RLO = 32
 JLO = 16
@@ -24,7 +25,7 @@
 
 def kernel(at_ref, ff_ref, sf_ref, out_ref,
            s_vmem, abuf, bbuf, left, acc, own_send, own_part, z_send, z_recv, lhs,
-           local_sem, ready, b_send, b_recv, a_send, a_recv, r_sems, own_sems, z_out, z_in):
+           local_sem, ready, late_in, b_send, b_recv, a_send, a_recv, r_sems, own_sems, z_out, z_in):
     grid = lax.axis_index("grid")
     depth = lax.axis_index("depth")
     x = depth // 4
@@ -63,22 +64,51 @@
     z_copies = [[remote(z_send.at[c, h], z_recv.at[h], z_out.at[2 * h + c], z_in.at[h], z_device(c)) for c in range(2)]
                 for h in range(2)]
 
+    def target(dx):
+        return lax.rem(x + dx, XS)
+
+    def signal(sem, to):
+        pl.semaphore_signal(sem, inc=1, device_id=to, device_id_type=MESH)
+
+    def when_start(condition, copy):
+        @pl.when(condition)
+        def _():
+            copy.start()
+
+    def push(c, late):
+        copies = [(dx, b_copy(c, dx, p)) for dx, p in ((1, 0), (3, 1))]
+        copies += [(dx, a_copy(c, 0, dx)) for dx in (1, 3, 2)]
+        copies += [(dx, b_copy(c, dx, p)) for dx, p in ((1, 1), (3, 0))]
+        for dx, copy in copies:
+            when_start((target(dx) == LATE) == late, copy)
+
     @pl.when(core == 0)
     def _():
-        pl.semaphore_wait(barrier, 5)
-        for dx, p in ((1, 0), (3, 1)):
-            b_copy(0, dx, p).start()
-        for to in (device(0, 1), z_device(1)):
-            pl.semaphore_signal(ready, inc=1, device_id=to, device_id_type=MESH)
-        for dx in (1, 3, 2):
-            a_copy(0, 0, dx).start()
-        for dx, p in ((1, 1), (3, 0)):
-            b_copy(0, dx, p).start()
+        @pl.when(x != LATE)
+        def _():
+            signal(barrier, (grid, (LATE * 2 + zl) * 2 + 1))
+            pl.semaphore_wait(barrier, 4)
+
+        @pl.when(x == LATE)
+        def _():
+            pl.semaphore_wait(barrier, 5)
+
+        push(0, False)
+        signal(ready, device(0, 1))
+        signal(ready, z_device(1))
         b_own.start()
         a_own[0].start()
         a_own[1].start()
         for dx in (1, 3, 2):
-            a_copy(0, 1, dx).start()
+            when_start(target(dx) != LATE, a_copy(0, 1, dx))
+
+        @pl.when(x != LATE)
+        def _():
+            pl.semaphore_wait(late_in, 1)
+
+        push(0, True)
+        for dx in (1, 3, 2):
+            when_start(target(dx) == LATE, a_copy(0, 1, dx))
         load_s.start()
         for dx in (1, 3):
             for p in range(2):
@@ -108,10 +138,19 @@
 
     @pl.when(core == 1)
     def _():
-        for to in [device(dx, 1) for dx in (1, 3, 2)] + [z_device(1)]:
-            pl.semaphore_signal(barrier, inc=1, device_id=to, device_id_type=MESH)
-        for to in [device(dx, 0) for dx in range(XS)] + [z_device(0)]:
-            pl.semaphore_signal(barrier, inc=1, device_id=to, device_id_type=MESH)
+        @pl.when(x != LATE)
+        def _():
+            for dx in (1, 3, 2):
+                signal(barrier, device(dx, 1))
+            for dx in range(XS):
+                signal(barrier, device(dx, 0))
+
+        @pl.when(x == LATE)
+        def _():
+            signal(barrier, device(0, 0))
+
+        signal(barrier, z_device(1))
+        signal(barrier, z_device(0))
         load_b = pltpu.make_async_copy(ff_ref, bbuf.at[1, 0], local_sem.at[0])
         load_a = [pltpu.make_async_copy(at_ref.at[:, :, rows_of(0, z_of[s])], abuf.at[s, 1, 0], local_sem.at[1 + s])
                   for s in range(2)]
@@ -119,23 +158,36 @@
                    remote(bbuf.at[c, 3, 1], bbuf.at[c, 2, 1], r_sems.at[0, 2 * c + 1], r_sems.at[1, 2 * c + 1], device(3, 1)))
                   for c in range(2)]
 
-        pl.semaphore_wait(barrier, 4)
-        for dx, p in ((1, 0), (3, 1)):
-            b_copy(1, dx, p).start()
-        for dx in (1, 3, 2):
-            a_copy(1, 0, dx).start()
-        for dx, p in ((1, 1), (3, 0)):
-            b_copy(1, dx, p).start()
+        @pl.when(x != LATE)
+        def _():
+            pl.semaphore_wait(barrier, 3)
+
+        @pl.when(x == LATE)
+        def _():
+            pl.semaphore_wait(barrier, 7)
+            for dx in (1, 3, 2):
+                signal(late_in, device(dx, 1))
+                signal(late_in, device(dx, 0))
+
+        push(1, False)
         load_b.start()
         load_a[0].start()
         load_a[1].start()
+        for dx in (1, 3, 2):
+            when_start((x != LATE) & (target(dx) != LATE), a_copy(1, 1, dx))
+
+        @pl.when(x != LATE)
+        def _():
+            pl.semaphore_wait(late_in, 1)
+
+        push(1, True)
         for c in (1, 0):
             b_copy(c, 1, 0).wait_recv()
             relays[c][0].start()
             b_copy(c, 3, 1).wait_recv()
             relays[c][1].start()
         for dx in (1, 3, 2):
-            a_copy(1, 1, dx).start()
+            when_start((x == LATE) | (target(dx) == LATE), a_copy(1, 1, dx))
         load_s.start()
         load_a[0].wait()
         weigh(0, 1, 0)
@@ -257,6 +309,7 @@
             pltpu.VMEM((2, 64, G2), BF16),
             pltpu.SemaphoreType.DMA((4,)),
             pltpu.SemaphoreType.REGULAR,
+            pltpu.SemaphoreType.REGULAR,
             pltpu.SemaphoreType.DMA((5,)),
             pltpu.SemaphoreType.DMA((9,)),
             pltpu.SemaphoreType.DMA((8,)),

time: 21 us -> 22.1 us (1.052)
  the two profiles are of different devices: /device:TPU:1 before, /device:TPU:69 now
where the time goes in v8:
time: 22.1 us; the launch traced here: 22 us
  Pallas kernels  21.3 us (96%)
  local copies, waits for them, and re-layouts  0.63 us (3%)
    pallas_call x1, Pallas kernels, on_device(): pl.pallas_call(kernel, out_shape=pltpu.VMEM((2, 2, JLO, M), BF16), in_spe...  21.3 us
    unnamed x1, local copies, waits for them, and re-layouts  0.63 us

profile of v8, /device:TPU:69, one launch (start us, length us, event | category | flops | bytes accessed | tf_op | source)
XLA Modules:
  0.0 22.0 jit_solution(17283262164398241324)
XLA Ops:
  0.0 21.3 %shard_map.37 = bf16[2,2,16,512]{3,2,1,0:T(8,128)(2,1)S(1)} custom-call(bf16[2,64,1024]{2,1,0:T(8,128)(2,1)} %bitcast.1, bf16[2,64,512]{2,1,0:T(8,128)(2,1)} %ff_ref.1, bf16[2,1024,512]{2,1,0:T(8,128)(2,1)} %sf_ref.1), custom_call_target="tpu_custom_call" | custom-call | flops 800000000 | bytes 2600000 | tf_op jit(solution)/shard_map/pallas_call | solution.py:294
  21.3 0.6 %copy.5 = bf16[2,2,16,512]{3,2,1,0:T(8,128)(2,1)} copy(bf16[2,2,16,512]{3,2,1,0:T(8,128)(2,1)S(1)} %shard_map.37) | data formatting | bytes 131072

commit v9 on v7

--- a/solution.py
+++ b/solution.py
@@ -161,7 +161,7 @@
         pl.semaphore_wait(ready, 2)
         for h in range(2):
             total = acc[h] + contract(0, h, 6, 8)
-            for c in range(2):
+            for c in (1, 0):
                 z_send[c, h] = total[c * 128:(c + 1) * 128].astype(BF16)
                 z_copies[h][c].start()
         load_a[1].wait()

time: 21 us -> 20.3 us (0.967)
  Pallas kernels: 20.2 us -> 19.6 us
    pallas_call x1, Pallas kernels: 20.2 us -> 19.6 us  [on_device(): pl.pallas_call(kernel, out_shape=pltpu.VMEM((2, 2, JLO, M), BF16), in_spe...]
where the time goes in v9:
time: 20.3 us; the launch traced here: 20.2 us
  Pallas kernels  19.6 us (97%)
  local copies, waits for them, and re-layouts  0.63 us (3%)
    pallas_call x1, Pallas kernels, on_device(): pl.pallas_call(kernel, out_shape=pltpu.VMEM((2, 2, JLO, M), BF16), in_spe...  19.6 us
    unnamed x1, local copies, waits for them, and re-layouts  0.63 us

profile of v9, /device:TPU:1, one launch (start us, length us, event | category | flops | bytes accessed | tf_op | source)
XLA Modules:
  0.0 20.2 jit_solution(15912175712001756273)
XLA Ops:
  0.0 19.6 %shard_map.37 = bf16[2,2,16,512]{3,2,1,0:T(8,128)(2,1)S(1)} custom-call(bf16[2,64,1024]{2,1,0:T(8,128)(2,1)} %bitcast.1, bf16[2,64,512]{2,1,0:T(8,128)(2,1)} %ff_ref.1, bf16[2,1024,512]{2,1,0:T(8,128)(2,1)} %sf_ref.1), custom_call_target="tpu_custom_call" | custom-call | flops 800000000 | bytes 2600000 | tf_op jit(solution)/shard_map/pallas_call | solution.py:242
  19.6 0.6 %copy.5 = bf16[2,2,16,512]{3,2,1,0:T(8,128)(2,1)} copy(bf16[2,2,16,512]{3,2,1,0:T(8,128)(2,1)S(1)} %shard_map.37) | data formatting | bytes 131072

commit v10 on v9

--- a/solution.py
+++ b/solution.py
@@ -115,9 +115,13 @@
         load_b = pltpu.make_async_copy(ff_ref, bbuf.at[1, 0], local_sem.at[0])
         load_a = [pltpu.make_async_copy(at_ref.at[:, :, rows_of(0, z_of[s])], abuf.at[s, 1, 0], local_sem.at[1 + s])
                   for s in range(2)]
-        relays = [(remote(bbuf.at[c, 1, 0], bbuf.at[c, 2, 0], r_sems.at[0, 2 * c], r_sems.at[1, 2 * c], device(1, 1)),
-                   remote(bbuf.at[c, 3, 1], bbuf.at[c, 2, 1], r_sems.at[0, 2 * c + 1], r_sems.at[1, 2 * c + 1], device(3, 1)))
-                  for c in range(2)]
+        def relay(c, h):
+            where = pl.ds(h * CJ, CJ)
+            i = 4 * h + 2 * c
+            return (remote(bbuf.at[c, 1, 0, :, where], bbuf.at[c, 2, 0, :, where], r_sems.at[0, i], r_sems.at[1, i], device(1, 1)),
+                    remote(bbuf.at[c, 3, 1, :, where], bbuf.at[c, 2, 1, :, where], r_sems.at[0, i + 1], r_sems.at[1, i + 1], device(3, 1)))
+
+        relays = [[relay(c, h) for c in range(2)] for h in range(2)]
 
         pl.semaphore_wait(barrier, 4)
         for dx, p in ((1, 0), (3, 1)):
@@ -131,9 +135,12 @@
         load_a[1].start()
         for c in (1, 0):
             b_copy(c, 1, 0).wait_recv()
-            relays[c][0].start()
+            relays[0][c][0].start()
             b_copy(c, 3, 1).wait_recv()
-            relays[c][1].start()
+            relays[0][c][1].start()
+        for c in (1, 0):
+            for copy in relays[1][c]:
+                copy.start()
         for dx in (1, 3, 2):
             a_copy(1, 1, dx).start()
         load_s.start()
@@ -155,11 +162,11 @@
         for c in (1, 0):
             a_copy(c, 0, 2).wait_recv()
             weigh(0, c, 2)
-        for c in (1, 0):
-            relays[c][0].wait_recv()
-            relays[c][1].wait_recv()
         pl.semaphore_wait(ready, 2)
         for h in range(2):
+            for c in (1, 0):
+                for copy in relays[h][c]:
+                    copy.wait_recv()
             total = acc[h] + contract(0, h, 6, 8)
             for c in (1, 0):
                 z_send[c, h] = total[c * 128:(c + 1) * 128].astype(BF16)
@@ -188,9 +195,9 @@
         for s in range(2):
             for dx in (1, 3, 2):
                 a_copy(1, s, dx).wait_send()
-        for c in range(2):
-            relays[c][0].wait_send()
-            relays[c][1].wait_send()
+        for copies in relays[0] + relays[1]:
+            for copy in copies:
+                copy.wait_send()
 
     def swap(v, tile_bit, lane_bit):
         step, width = 1 << tile_bit, 1 << lane_bit
@@ -261,7 +268,7 @@
             pltpu.SemaphoreType.DMA((9,)),
             pltpu.SemaphoreType.DMA((8,)),
             pltpu.SemaphoreType.DMA((14,)),
-            pltpu.SemaphoreType.DMA((2, 4)),
+            pltpu.SemaphoreType.DMA((2, 8)),
             pltpu.SemaphoreType.DMA((2, 2)),
             pltpu.SemaphoreType.DMA((4,)),
             pltpu.SemaphoreType.DMA((2,)),

time: 20.3 us -> 19.6 us (0.966)
  Pallas kernels: 19.6 us -> 18.8 us
    pallas_call x1, Pallas kernels: 19.6 us -> 18.8 us  [on_device(): pl.pallas_call(kernel, out_shape=pltpu.VMEM((2, 2, JLO, M), BF16), in_spe...]
where the time goes in v10:
time: 19.6 us; the launch traced here: 19.5 us
  Pallas kernels  18.8 us (96%)
  local copies, waits for them, and re-layouts  0.63 us (3%)
    pallas_call x1, Pallas kernels, on_device(): pl.pallas_call(kernel, out_shape=pltpu.VMEM((2, 2, JLO, M), BF16), in_spe...  18.8 us
    unnamed x1, local copies, waits for them, and re-layouts  0.63 us

profile of v10, /device:TPU:1, one launch (start us, length us, event | category | flops | bytes accessed | tf_op | source)
XLA Modules:
  0.0 19.5 jit_solution(11418171110939494937)
XLA Ops:
  0.0 18.8 %shard_map.37 = bf16[2,2,16,512]{3,2,1,0:T(8,128)(2,1)S(1)} custom-call(bf16[2,64,1024]{2,1,0:T(8,128)(2,1)} %bitcast.1, bf16[2,64,512]{2,1,0:T(8,128)(2,1)} %ff_ref.1, bf16[2,1024,512]{2,1,0:T(8,128)(2,1)} %sf_ref.1), custom_call_target="tpu_custom_call" | custom-call | flops 800000000 | bytes 2600000 | tf_op jit(solution)/shard_map/pallas_call | solution.py:249
  18.8 0.6 %copy.5 = bf16[2,2,16,512]{3,2,1,0:T(8,128)(2,1)} copy(bf16[2,2,16,512]{3,2,1,0:T(8,128)(2,1)S(1)} %shard_map.37) | data formatting | bytes 131072

commit v11 on v10

--- a/solution.py
+++ b/solution.py
@@ -48,15 +48,21 @@
     load_s = pltpu.make_async_copy(sf_ref, s_vmem, local_sem.at[3])
     barrier = pltpu.get_barrier_semaphore()
 
-    def b_copy(c, dx, p):
-        i = (0 if dx == 1 else 2) + p
-        return remote(ff_ref.at[p], bbuf.at[c, dx, p], b_send.at[i], b_recv.at[c * 4 + i], device(dx, 1))
+    halves = [pl.ds(h * CJ, CJ) for h in range(2)]
+
+    def b_copy(c, dx):
+        p, i = (0, 0) if dx == 1 else (1, 1)
+        return remote(ff_ref.at[p], bbuf.at[c, dx, p], b_send.at[i], b_recv.at[c * 6 + i], device(dx, 1))
+
+    def b_rest(c, dx, h):
+        p, i = (1, 2 + h) if dx == 1 else (0, 4 + h)
+        return remote(ff_ref.at[p, :, halves[h]], bbuf.at[c, dx, p, :, halves[h]], b_send.at[i], b_recv.at[c * 6 + i], device(dx, 1))
 
     def a_copy(c, s, dx):
         i = s * 3 + dx - 1
         return remote(at_ref.at[:, :, rows_of(dx, z_of[s])], abuf.at[s, c, dx], a_send.at[i], a_recv.at[c * 6 + i], device(dx, 1))
 
-    b_own = remote(ff_ref, bbuf.at[0, 0], b_send.at[4], b_recv.at[8], device(0, 1))
+    b_own = remote(ff_ref, bbuf.at[0, 0], b_send.at[6], b_recv.at[12], device(0, 1))
     a_own = [remote(at_ref.at[:, :, rows_of(0, z_of[s])], abuf.at[s, 0, 0], a_send.at[6 + s], a_recv.at[12 + s], device(0, 1))
              for s in range(2)]
     own_copies = [remote(own_send.at[h], own_part.at[h], own_sems.at[0, h], own_sems.at[1, h], device(0, 0)) for h in range(2)]
@@ -66,23 +72,26 @@
     @pl.when(core == 0)
     def _():
         pl.semaphore_wait(barrier, 5)
-        for dx, p in ((1, 0), (3, 1)):
-            b_copy(0, dx, p).start()
+        for dx in (1, 3):
+            b_copy(0, dx).start()
         for to in (device(0, 1), z_device(1)):
             pl.semaphore_signal(ready, inc=1, device_id=to, device_id_type=MESH)
         for dx in (1, 3, 2):
             a_copy(0, 0, dx).start()
-        for dx, p in ((1, 1), (3, 0)):
-            b_copy(0, dx, p).start()
+        for dx in (1, 3):
+            b_rest(0, dx, 0).start()
         b_own.start()
         a_own[0].start()
+        for dx in (1, 3):
+            b_rest(0, dx, 1).start()
         a_own[1].start()
         for dx in (1, 3, 2):
             a_copy(0, 1, dx).start()
         load_s.start()
         for dx in (1, 3):
-            for p in range(2):
-                b_copy(0, dx, p).wait_send()
+            b_copy(0, dx).wait_send()
+            for h in range(2):
+                b_rest(0, dx, h).wait_send()
         for s in range(2):
             for dx in (1, 3, 2):
                 a_copy(0, s, dx).wait_send()
@@ -124,20 +133,22 @@
         relays = [[relay(c, h) for c in range(2)] for h in range(2)]
 
         pl.semaphore_wait(barrier, 4)
-        for dx, p in ((1, 0), (3, 1)):
-            b_copy(1, dx, p).start()
+        for dx in (1, 3):
+            b_copy(1, dx).start()
         for dx in (1, 3, 2):
             a_copy(1, 0, dx).start()
-        for dx, p in ((1, 1), (3, 0)):
-            b_copy(1, dx, p).start()
+        for dx in (1, 3):
+            b_rest(1, dx, 0).start()
         load_b.start()
         load_a[0].start()
         load_a[1].start()
         for c in (1, 0):
-            b_copy(c, 1, 0).wait_recv()
+            b_copy(c, 1).wait_recv()
             relays[0][c][0].start()
-            b_copy(c, 3, 1).wait_recv()
+            b_copy(c, 3).wait_recv()
             relays[0][c][1].start()
+        for dx in (1, 3):
+            b_rest(1, dx, 1).start()
         for c in (1, 0):
             for copy in relays[1][c]:
                 copy.start()
@@ -154,16 +165,21 @@
         weigh(0, 0, 0)
         load_b.wait()
         b_own.wait_recv()
-        for c in (1, 0):
-            b_copy(c, 1, 1).wait_recv()
-            b_copy(c, 3, 0).wait_recv()
-        for h in range(2):
+
+        def early(h):
+            for c in (1, 0):
+                for dx in (1, 3):
+                    b_rest(c, dx, h).wait_recv()
             acc[h] = contract(0, h, 0, 6)
+
+        early(0)
         for c in (1, 0):
             a_copy(c, 0, 2).wait_recv()
             weigh(0, c, 2)
         pl.semaphore_wait(ready, 2)
         for h in range(2):
+            if h == 1:
+                early(1)
             for c in (1, 0):
                 for copy in relays[h][c]:
                     copy.wait_recv()
@@ -190,8 +206,9 @@
             own_copies[h].start()
             own_part[h] = total[128:].astype(BF16)
         for dx in (1, 3):
-            for p in range(2):
-                b_copy(1, dx, p).wait_send()
+            b_copy(1, dx).wait_send()
+            for h in range(2):
+                b_rest(1, dx, h).wait_send()
         for s in range(2):
             for dx in (1, 3, 2):
                 a_copy(1, s, dx).wait_send()
@@ -264,8 +281,8 @@
             pltpu.VMEM((2, 64, G2), BF16),
             pltpu.SemaphoreType.DMA((4,)),
             pltpu.SemaphoreType.REGULAR,
-            pltpu.SemaphoreType.DMA((5,)),
-            pltpu.SemaphoreType.DMA((9,)),
+            pltpu.SemaphoreType.DMA((7,)),
+            pltpu.SemaphoreType.DMA((13,)),
             pltpu.SemaphoreType.DMA((8,)),
             pltpu.SemaphoreType.DMA((14,)),
             pltpu.SemaphoreType.DMA((2, 8)),

time: 19.6 us -> 20.1 us (1.026)
  Pallas kernels: 18.8 us -> 19.4 us
    pallas_call x1, Pallas kernels: 18.8 us -> 19.4 us  [on_device(): pl.pallas_call(kernel, out_shape=pltpu.VMEM((2, 2, JLO, M), BF16), in_spe...]
where the time goes in v11:
time: 20.1 us; the launch traced here: 20 us
  Pallas kernels  19.4 us (97%)
  local copies, waits for them, and re-layouts  0.63 us (3%)
    pallas_call x1, Pallas kernels, on_device(): pl.pallas_call(kernel, out_shape=pltpu.VMEM((2, 2, JLO, M), BF16), in_spe...  19.4 us
    unnamed x1, local copies, waits for them, and re-layouts  0.63 us

profile of v11, /device:TPU:1, one launch (start us, length us, event | category | flops | bytes accessed | tf_op | source)
XLA Modules:
  0.0 20.0 jit_solution(7806684560124254044)
XLA Ops:
  0.0 19.4 %shard_map.37 = bf16[2,2,16,512]{3,2,1,0:T(8,128)(2,1)S(1)} custom-call(bf16[2,64,1024]{2,1,0:T(8,128)(2,1)} %bitcast.1, bf16[2,64,512]{2,1,0:T(8,128)(2,1)} %ff_ref.1, bf16[2,1024,512]{2,1,0:T(8,128)(2,1)} %sf_ref.1), custom_call_target="tpu_custom_call" | custom-call | flops 800000000 | bytes 2600000 | tf_op jit(solution)/shard_map/pallas_call | solution.py:266
  19.4 0.6 %copy.5 = bf16[2,2,16,512]{3,2,1,0:T(8,128)(2,1)} copy(bf16[2,2,16,512]{3,2,1,0:T(8,128)(2,1)S(1)} %shard_map.37) | data formatting | bytes 131072

commit v12 on v11

--- a/solution.py
+++ b/solution.py
@@ -142,16 +142,36 @@
         load_b.start()
         load_a[0].start()
         load_a[1].start()
-        for c in (1, 0):
-            b_copy(c, 1).wait_recv()
-            relays[0][c][0].start()
-            b_copy(c, 3).wait_recv()
-            relays[0][c][1].start()
-        for dx in (1, 3):
-            b_rest(1, dx, 1).start()
-        for c in (1, 0):
-            for copy in relays[1][c]:
-                copy.start()
+
+        def serve(first):
+            steps = (first, 4 - first)
+            way = {1: 0, 3: 1}
+
+            def pass_on(c, dx, h):
+                relays[h][c][way[dx]].start()
+
+            for dx in steps:
+                b_copy(1, dx).wait_recv()
+                pass_on(1, dx, 0)
+            b_copy(0, first).wait_recv()
+            pass_on(0, first, 0)
+            for dx in (1, 3):
+                b_rest(1, dx, 1).start()
+            pass_on(1, first, 1)
+            pass_on(0, first, 1)
+            pass_on(1, steps[1], 1)
+            b_copy(0, steps[1]).wait_recv()
+            pass_on(0, steps[1], 0)
+            pass_on(0, steps[1], 1)
+
+        @pl.when(x == 1)
+        def _():
+            serve(3)
+
+        @pl.when(x != 1)
+        def _():
+            serve(1)
+
         for dx in (1, 3, 2):
             a_copy(1, 1, dx).start()
         load_s.start()

time: 20.1 us -> 19 us (0.945)
  Pallas kernels: 19.4 us -> 18.3 us
    pallas_call x1, Pallas kernels: 19.4 us -> 18.3 us  [on_device(): pl.pallas_call(kernel, out_shape=pltpu.VMEM((2, 2, JLO, M), BF16), in_spe...]
where the time goes in v12:
time: 19 us; the launch traced here: 18.9 us
  Pallas kernels  18.3 us (96%)
  local copies, waits for them, and re-layouts  0.63 us (3%)
    pallas_call x1, Pallas kernels, on_device(): pl.pallas_call(kernel, out_shape=pltpu.VMEM((2, 2, JLO, M), BF16), in_spe...  18.3 us
    unnamed x1, local copies, waits for them, and re-layouts  0.63 us

profile of v12, /device:TPU:1, one launch (start us, length us, event | category | flops | bytes accessed | tf_op | source)
XLA Modules:
  0.0 18.9 jit_solution(11924423655681708166)
XLA Ops:
  0.0 18.3 %shard_map.37 = bf16[2,2,16,512]{3,2,1,0:T(8,128)(2,1)S(1)} custom-call(bf16[2,64,1024]{2,1,0:T(8,128)(2,1)} %bitcast.1, bf16[2,64,512]{2,1,0:T(8,128)(2,1)} %ff_ref.1, bf16[2,1024,512]{2,1,0:T(8,128)(2,1)} %sf_ref.1), custom_call_target="tpu_custom_call" | custom-call | flops 800000000 | bytes 2600000 | tf_op jit(solution)/shard_map/pallas_call | solution.py:286
  18.3 0.6 %copy.5 = bf16[2,2,16,512]{3,2,1,0:T(8,128)(2,1)} copy(bf16[2,2,16,512]{3,2,1,0:T(8,128)(2,1)S(1)} %shard_map.37) | data formatting | bytes 131072

commit v13 on v12

--- a/solution.py
+++ b/solution.py
@@ -110,10 +110,10 @@
             left[s, pl.ds(side * 128, 64), lanes] = value * minus
             left[s, pl.ds(side * 128 + 64, 64), lanes] = pltpu.roll(value, KH, 1)
 
-    def contract(s, h, first, last):
+    def contract(s, h, first, last, rows=slice(0, 256)):
         where = pl.ds(h * CJ, CJ)
         right = jnp.concatenate([bbuf[c, slot, :, :, where].reshape(KB, CJ) for c, slot in order[first:last]], axis=0)
-        return jnp.dot(left[s, :, pl.ds(first * KB, (last - first) * KB)], right, preferred_element_type=F32)
+        return jnp.dot(left[s, rows, pl.ds(first * KB, (last - first) * KB)], right, preferred_element_type=F32)
 
     @pl.when(core == 1)
     def _():
@@ -221,10 +221,10 @@
             a_copy(c, 1, 2).wait_recv()
             weigh(1, c, 2)
         for h in range(2):
-            total = acc[h] + contract(1, h, 6, 8)
-            own_send[h] = total[:128].astype(BF16)
+            own_send[h] = (acc[h, :128] + contract(1, h, 6, 8, slice(0, 128))).astype(BF16)
             own_copies[h].start()
-            own_part[h] = total[128:].astype(BF16)
+        for h in range(2):
+            own_part[h] = (acc[h, 128:] + contract(1, h, 6, 8, slice(128, 256))).astype(BF16)
         for dx in (1, 3):
             b_copy(1, dx).wait_send()
             for h in range(2):

time: 19 us -> 19 us (level)
  no operation moved by 1% of the time
where the time goes in v13:
time: 19 us; the launch traced here: 18.9 us
  Pallas kernels  18.3 us (96%)
  local copies, waits for them, and re-layouts  0.63 us (3%)
    pallas_call x1, Pallas kernels, on_device(): pl.pallas_call(kernel, out_shape=pltpu.VMEM((2, 2, JLO, M), BF16), in_spe...  18.3 us
    unnamed x1, local copies, waits for them, and re-layouts  0.63 us

profile of v13, /device:TPU:1, one launch (start us, length us, event | category | flops | bytes accessed | tf_op | source)
XLA Modules:
  0.0 18.9 jit_solution(3924057484048276740)
XLA Ops:
  0.0 18.3 %shard_map.37 = bf16[2,2,16,512]{3,2,1,0:T(8,128)(2,1)S(1)} custom-call(bf16[2,64,1024]{2,1,0:T(8,128)(2,1)} %bitcast.1, bf16[2,64,512]{2,1,0:T(8,128)(2,1)} %ff_ref.1, bf16[2,1024,512]{2,1,0:T(8,128)(2,1)} %sf_ref.1), custom_call_target="tpu_custom_call" | custom-call | flops 800000000 | bytes 2600000 | tf_op jit(solution)/shard_map/pallas_call | solution.py:286
  18.3 0.6 %copy.5 = bf16[2,2,16,512]{3,2,1,0:T(8,128)(2,1)} copy(bf16[2,2,16,512]{3,2,1,0:T(8,128)(2,1)S(1)} %shard_map.37) | data formatting | bytes 131072

commit v14 on v12

--- a/solution.py
+++ b/solution.py
@@ -204,7 +204,7 @@
                 for copy in relays[h][c]:
                     copy.wait_recv()
             total = acc[h] + contract(0, h, 6, 8)
-            for c in (1, 0):
+            for c in ((1, 0), (0, 1))[h]:
                 z_send[c, h] = total[c * 128:(c + 1) * 128].astype(BF16)
                 z_copies[h][c].start()
         load_a[1].wait()

time: 19 us -> 19.7 us (1.037)
  Pallas kernels: 18.3 us -> 18.9 us
    pallas_call x1, Pallas kernels: 18.3 us -> 18.9 us  [on_device(): pl.pallas_call(kernel, out_shape=pltpu.VMEM((2, 2, JLO, M), BF16), in_spe...]
where the time goes in v14:
time: 19.7 us; the launch traced here: 19.6 us
  Pallas kernels  18.9 us (96%)
  local copies, waits for them, and re-layouts  0.63 us (3%)
    pallas_call x1, Pallas kernels, on_device(): pl.pallas_call(kernel, out_shape=pltpu.VMEM((2, 2, JLO, M), BF16), in_spe...  18.9 us
    unnamed x1, local copies, waits for them, and re-layouts  0.63 us

profile of v14, /device:TPU:1, one launch (start us, length us, event | category | flops | bytes accessed | tf_op | source)
XLA Modules:
  0.0 19.6 jit_solution(2730530510868223670)
XLA Ops:
  0.0 18.9 %shard_map.37 = bf16[2,2,16,512]{3,2,1,0:T(8,128)(2,1)S(1)} custom-call(bf16[2,64,1024]{2,1,0:T(8,128)(2,1)} %bitcast.1, bf16[2,64,512]{2,1,0:T(8,128)(2,1)} %ff_ref.1, bf16[2,1024,512]{2,1,0:T(8,128)(2,1)} %sf_ref.1), custom_call_target="tpu_custom_call" | custom-call | flops 800000000 | bytes 2600000 | tf_op jit(solution)/shard_map/pallas_call | solution.py:286
  18.9 0.6 %copy.5 = bf16[2,2,16,512]{3,2,1,0:T(8,128)(2,1)} copy(bf16[2,2,16,512]{3,2,1,0:T(8,128)(2,1)S(1)} %shard_map.37) | data formatting | bytes 131072

commit v15 on v12

--- a/solution.py
+++ b/solution.py
@@ -76,7 +76,7 @@
             b_copy(0, dx).start()
         for to in (device(0, 1), z_device(1)):
             pl.semaphore_signal(ready, inc=1, device_id=to, device_id_type=MESH)
-        for dx in (1, 3, 2):
+        for dx in (2, 1, 3):
             a_copy(0, 0, dx).start()
         for dx in (1, 3):
             b_rest(0, dx, 0).start()
@@ -135,7 +135,7 @@
         pl.semaphore_wait(barrier, 4)
         for dx in (1, 3):
             b_copy(1, dx).start()
-        for dx in (1, 3, 2):
+        for dx in (2, 1, 3):
             a_copy(1, 0, dx).start()
         for dx in (1, 3):
             b_rest(1, dx, 0).start()

time: 19 us -> 19.2 us (1.011); the launches traced: 18.9 us -> 18.9 us
  no operation moved by 1% of the time
where the time goes in v15:
time: 19.2 us; the launch traced here: 18.9 us
  Pallas kernels  18.3 us (95%)
  local copies, waits for them, and re-layouts  0.63 us (3%)
    pallas_call x1, Pallas kernels, on_device(): pl.pallas_call(kernel, out_shape=pltpu.VMEM((2, 2, JLO, M), BF16), in_spe...  18.3 us
    unnamed x1, local copies, waits for them, and re-layouts  0.63 us

profile of v15, /device:TPU:1, one launch (start us, length us, event | category | flops | bytes accessed | tf_op | source)
XLA Modules:
  0.0 18.9 jit_solution(2883946363775436712)
XLA Ops:
  0.0 18.3 %shard_map.37 = bf16[2,2,16,512]{3,2,1,0:T(8,128)(2,1)S(1)} custom-call(bf16[2,64,1024]{2,1,0:T(8,128)(2,1)} %bitcast.1, bf16[2,64,512]{2,1,0:T(8,128)(2,1)} %ff_ref.1, bf16[2,1024,512]{2,1,0:T(8,128)(2,1)} %sf_ref.1), custom_call_target="tpu_custom_call" | custom-call | flops 800000000 | bytes 2600000 | tf_op jit(solution)/shard_map/pallas_call | solution.py:286
  18.3 0.6 %copy.5 = bf16[2,2,16,512]{3,2,1,0:T(8,128)(2,1)} copy(bf16[2,2,16,512]{3,2,1,0:T(8,128)(2,1)S(1)} %shard_map.37) | data formatting | bytes 131072

commit v16 on v14

--- a/solution.py
+++ b/solution.py
@@ -110,10 +110,10 @@
             left[s, pl.ds(side * 128, 64), lanes] = value * minus
             left[s, pl.ds(side * 128 + 64, 64), lanes] = pltpu.roll(value, KH, 1)
 
-    def contract(s, h, first, last):
+    def contract(s, h, first, last, rows=slice(0, 256)):
         where = pl.ds(h * CJ, CJ)
         right = jnp.concatenate([bbuf[c, slot, :, :, where].reshape(KB, CJ) for c, slot in order[first:last]], axis=0)
-        return jnp.dot(left[s, :, pl.ds(first * KB, (last - first) * KB)], right, preferred_element_type=F32)
+        return jnp.dot(left[s, rows, pl.ds(first * KB, (last - first) * KB)], right, preferred_element_type=F32)
 
     @pl.when(core == 1)
     def _():
@@ -203,10 +203,18 @@
             for c in (1, 0):
                 for copy in relays[h][c]:
                     copy.wait_recv()
-            total = acc[h] + contract(0, h, 6, 8)
-            for c in ((1, 0), (0, 1))[h]:
-                z_send[c, h] = total[c * 128:(c + 1) * 128].astype(BF16)
-                z_copies[h][c].start()
+
+            def send(cores, h=h):
+                for c in cores:
+                    rows = slice(c * 128, (c + 1) * 128)
+                    z_send[c, h] = (acc[h, rows] + contract(0, h, 6, 8, rows)).astype(BF16)
+                    z_copies[h][c].start()
+
+            if h == 0:
+                send((1, 0))
+            else:
+                pl.when(x == 0)(lambda: send((1, 0)))
+                pl.when(x != 0)(lambda: send((0, 1)))
         load_a[1].wait()
         weigh(1, 1, 0)
         a_own[1].wait_recv()

time: 19.7 us -> 19 us (0.964)
  Pallas kernels: 18.9 us -> 18.2 us
    pallas_call x1, Pallas kernels: 18.9 us -> 18.2 us  [on_device(): pl.pallas_call(kernel, out_shape=pltpu.VMEM((2, 2, JLO, M), BF16), in_spe...]
where the time goes in v16:
time: 19 us; the launch traced here: 18.9 us
  Pallas kernels  18.2 us (96%)
  local copies, waits for them, and re-layouts  0.63 us (3%)
    pallas_call x1, Pallas kernels, on_device(): pl.pallas_call(kernel, out_shape=pltpu.VMEM((2, 2, JLO, M), BF16), in_spe...  18.2 us
    unnamed x1, local copies, waits for them, and re-layouts  0.63 us

profile of v16, /device:TPU:1, one launch (start us, length us, event | category | flops | bytes accessed | tf_op | source)
XLA Modules:
  0.0 18.9 jit_solution(3680776209789909409)
XLA Ops:
  0.0 18.2 %shard_map.37 = bf16[2,2,16,512]{3,2,1,0:T(8,128)(2,1)S(1)} custom-call(bf16[2,64,1024]{2,1,0:T(8,128)(2,1)} %bitcast.1, bf16[2,64,512]{2,1,0:T(8,128)(2,1)} %ff_ref.1, bf16[2,1024,512]{2,1,0:T(8,128)(2,1)} %sf_ref.1), custom_call_target="tpu_custom_call" | custom-call | flops 800000000 | bytes 2600000 | tf_op jit(solution)/shard_map/pallas_call | solution.py:294
  18.3 0.6 %copy.5 = bf16[2,2,16,512]{3,2,1,0:T(8,128)(2,1)} copy(bf16[2,2,16,512]{3,2,1,0:T(8,128)(2,1)S(1)} %shard_map.37) | data formatting | bytes 131072

commit v17 on v12

--- a/solution.py
+++ b/solution.py
@@ -78,10 +78,10 @@
             pl.semaphore_signal(ready, inc=1, device_id=to, device_id_type=MESH)
         for dx in (1, 3, 2):
             a_copy(0, 0, dx).start()
-        for dx in (1, 3):
-            b_rest(0, dx, 0).start()
         b_own.start()
         a_own[0].start()
+        for dx in (1, 3):
+            b_rest(0, dx, 0).start()
         for dx in (1, 3):
             b_rest(0, dx, 1).start()
         a_own[1].start()

time: 19 us -> 19 us (level)
  no operation moved by 1% of the time
where the time goes in v17:
time: 19 us; the launch traced here: 18.9 us
  Pallas kernels  18.3 us (96%)
  local copies, waits for them, and re-layouts  0.63 us (3%)
    pallas_call x1, Pallas kernels, on_device(): pl.pallas_call(kernel, out_shape=pltpu.VMEM((2, 2, JLO, M), BF16), in_spe...  18.3 us
    unnamed x1, local copies, waits for them, and re-layouts  0.63 us

profile of v17, /device:TPU:1, one launch (start us, length us, event | category | flops | bytes accessed | tf_op | source)
XLA Modules:
  0.0 18.9 jit_solution(13293334098301719346)
XLA Ops:
  0.0 18.3 %shard_map.37 = bf16[2,2,16,512]{3,2,1,0:T(8,128)(2,1)S(1)} custom-call(bf16[2,64,1024]{2,1,0:T(8,128)(2,1)} %bitcast.1, bf16[2,64,512]{2,1,0:T(8,128)(2,1)} %ff_ref.1, bf16[2,1024,512]{2,1,0:T(8,128)(2,1)} %sf_ref.1), custom_call_target="tpu_custom_call" | custom-call | flops 800000000 | bytes 2600000 | tf_op jit(solution)/shard_map/pallas_call | solution.py:286
  18.3 0.6 %copy.5 = bf16[2,2,16,512]{3,2,1,0:T(8,128)(2,1)} copy(bf16[2,2,16,512]{3,2,1,0:T(8,128)(2,1)S(1)} %shard_map.37) | data formatting | bytes 131072
